TPU v7x, 32 devices: a whole 2x2x4 slice. The times are simulated.
32 devices in a mesh: ctx: 8 (over z, x), head: 4 (over y, core).
Axes of the slice: x: 2, y: 2, z: 4, core: 2. Of those that a mesh axis runs over, the one named last changes fastest.
Arguments:
- tokens: bfloat16 [4096, 7168], P(('ctx', 'head')), may hold values from -6 to 6
- routes: int32 [4096, 8], P(('ctx', 'head')), may hold values from 0 to 255, all different within a row; in each aligned block of 128 rows (0 to 127, 128 to 255, ...) at most 6 rows name the same one
- route_weight: float32 [4096, 8], P(('ctx', 'head')), may hold values from 0.2 to 2
- w_gate: bfloat16 [8, 7168, 1024], P('ctx', 'head'), may hold values from -0.0625 to 0.0625
- w_up: bfloat16 [8, 7168, 1024], P('ctx', 'head'), may hold values from -0.0625 to 0.0625
- w_down: bfloat16 [8, 1024, 7168], P('ctx', None, 'head'), may hold values from -0.1875 to 0.1875
- grad_out: bfloat16 [4096, 7168], P(('ctx', 'head')), may hold values from -6 to 6
Outputs:
- moe_out: bfloat16 [4096, 7168], P(('ctx', 'head'))
- grad_tokens: bfloat16 [4096, 7168], P(('ctx', 'head'))
- grad_route: float32 [4096, 8], P(('ctx', 'head'))
- grad_gate: bfloat16 [8, 7168, 1024], P('ctx', 'head')
- grad_up: bfloat16 [8, 7168, 1024], P('ctx', 'head')
- grad_down: bfloat16 [8, 1024, 7168], P('ctx', None, 'head')
Inputs may be any that keep to these rules, and one draw needn't show every extreme that they name: `routes`: each row names 8 different experts. In each aligned block of 128 rows (the tokens of one device) no expert is named more than 6 times. Experts below 8 are the window's.
All inputs are finite; a program needn't handle non-finite values.
Results may differ from a plain program's by a relative error of at most 0.0057.
Values may be sent and summed in bfloat16 or wider, within the bound.
A program may use at most 128 MiB of HBM per device.

v0:
```python
import jax
import jax.numpy as jnp
from jax import lax
from jax.sharding import PartitionSpec as P

CAP = 6


def silu_parts(gate_pre):
    sigmoid_g = jax.nn.sigmoid(gate_pre)
    return (gate_pre * sigmoid_g, sigmoid_g * (1.0 + gate_pre * (1.0 - sigmoid_g)))


def activate(summed, hidden_width):
    gate_pre = summed[:, :hidden_width]
    up_value = summed[:, hidden_width : 2 * hidden_width]
    back_grad = summed[:, 2 * hidden_width :]
    smooth, silu_slope = silu_parts(gate_pre)
    hidden = (smooth * up_value).astype(jnp.bfloat16)
    d_gate = (back_grad * up_value * silu_slope).astype(jnp.bfloat16)
    d_up = (back_grad * smooth).astype(jnp.bfloat16)
    return jnp.concatenate([hidden, d_gate, d_up], axis=1)


def on_device(tokens, routes, route_weight, w_gate, w_up, w_down, grad_out):
    experts = lax.axis_size("ctx")
    groups = lax.axis_size("head")
    tok_rows, model_width = tokens.shape
    pick_count = routes.shape[1]
    slice_width = w_gate.shape[1]
    hidden_width = w_gate.shape[2]
    slot_count = experts * CAP
    flat_routes = routes.reshape(-1)
    onehot = (flat_routes[:, None] == jnp.arange(experts, dtype=jnp.int32)[None, :]).astype(
        jnp.int32
    )
    before = jnp.sum((jnp.cumsum(onehot, axis=0) - onehot) * onehot, axis=1)
    slot_of = jnp.where(flat_routes < experts, flat_routes * CAP + before, -1)
    placed = (slot_of[:, None] == jnp.arange(slot_count, dtype=jnp.int32)[None, :]).astype(
        jnp.float32
    )
    placed_picks = placed.reshape(tok_rows, pick_count, slot_count)
    selector = jnp.sum(placed_picks, axis=1)
    weighted_sel = jnp.sum(placed_picks * route_weight[:, :, None], axis=1)
    slot_weight = jnp.sum(weighted_sel, axis=0)
    stacked = jnp.concatenate([tokens, grad_out], axis=1)
    slot_values = jnp.dot(
        selector.T.astype(jnp.bfloat16), stacked, preferred_element_type=jnp.float32
    )
    x_rows = slot_values[:, :model_width].astype(jnp.bfloat16)
    dy_rows = slot_values[:, model_width:]
    do_rows = (slot_weight[:, None] * dy_rows).astype(jnp.bfloat16)

    def to_slices(block):
        return block.reshape(experts, CAP, groups, slice_width).transpose(0, 2, 1, 3)

    def to_tokens(block):
        return (
            block.reshape(experts, groups, CAP, slice_width)
            .transpose(0, 2, 1, 3)
            .reshape(slot_count, model_width)
        )

    total_rows = experts * groups * CAP
    x_in, d_in = (
        lax.all_to_all(
            to_slices(x_rows).reshape(experts * groups, CAP, slice_width),
            ("ctx", "head"),
            split_axis=0,
            concat_axis=0,
            tiled=True,
        ),
        lax.all_to_all(
            to_slices(do_rows).reshape(experts * groups, CAP, slice_width),
            ("ctx", "head"),
            split_axis=0,
            concat_axis=0,
            tiled=True,
        ),
    )
    x_in = x_in.reshape(total_rows, slice_width)
    d_in = d_in.reshape(total_rows, slice_width)
    gate_slice = w_gate[0]
    up_slice = w_up[0]
    down_slice = w_down[0]
    w_pair = jnp.concatenate([gate_slice, up_slice], axis=1)
    forward = jnp.dot(x_in, w_pair, preferred_element_type=jnp.float32)
    backward = lax.dot_general(
        d_in, down_slice, (((1,), (1,)), ((), ())), preferred_element_type=jnp.float32
    )
    row_share = lax.psum_scatter(
        jnp.concatenate([forward, backward], axis=1), "head", scatter_dimension=0, tiled=True
    )
    packed = lax.all_gather(activate(row_share, hidden_width), "head", axis=0, tiled=True)
    hidden = packed[:, :hidden_width]
    grads_hidden = packed[:, hidden_width:]
    expert_out = jnp.dot(hidden, down_slice, preferred_element_type=jnp.float32).astype(
        jnp.bfloat16
    )
    grad_down = lax.dot_general(
        hidden, d_in, (((0,), (0,)), ((), ())), preferred_element_type=jnp.float32
    ).astype(jnp.bfloat16)
    grad_pair = lax.dot_general(
        x_in, grads_hidden, (((0,), (0,)), ((), ())), preferred_element_type=jnp.float32
    )
    grad_gate = grad_pair[:, :hidden_width].astype(jnp.bfloat16)
    grad_up = grad_pair[:, hidden_width:].astype(jnp.bfloat16)
    grad_rows = lax.dot_general(
        grads_hidden, w_pair, (((1,), (1,)), ((), ())), preferred_element_type=jnp.float32
    ).astype(jnp.bfloat16)
    back_out, back_grad = (
        lax.all_to_all(
            expert_out.reshape(experts * groups, CAP, slice_width),
            ("ctx", "head"),
            split_axis=0,
            concat_axis=0,
            tiled=True,
        ),
        lax.all_to_all(
            grad_rows.reshape(experts * groups, CAP, slice_width),
            ("ctx", "head"),
            split_axis=0,
            concat_axis=0,
            tiled=True,
        ),
    )
    out_slots = to_tokens(back_out).astype(jnp.float32)
    grad_slots = to_tokens(back_grad)
    moe_out = jnp.dot(
        weighted_sel, out_slots, precision=lax.Precision.HIGHEST, preferred_element_type=jnp.float32
    ).astype(jnp.bfloat16)
    grad_tokens = jnp.dot(
        selector.astype(jnp.bfloat16), grad_slots, preferred_element_type=jnp.float32
    ).astype(jnp.bfloat16)
    slot_inner = jnp.sum(dy_rows * out_slots, axis=1)
    grad_route = jnp.dot(
        placed, slot_inner, precision=lax.Precision.HIGHEST, preferred_element_type=jnp.float32
    ).reshape(tok_rows, pick_count)
    return (moe_out, grad_tokens, grad_route, grad_gate[None], grad_up[None], grad_down[None])


def solution(mesh):
    return jax.shard_map(
        on_device,
        mesh=mesh,
        in_specs=(
            P(("ctx", "head"), None),
            P(("ctx", "head"), None),
            P(("ctx", "head"), None),
            P("ctx", "head", None),
            P("ctx", "head", None),
            P("ctx", None, "head"),
            P(("ctx", "head"), None),
        ),
        out_specs=(
            P(("ctx", "head"), None),
            P(("ctx", "head"), None),
            P(("ctx", "head"), None),
            P("ctx", "head", None),
            P("ctx", "head", None),
            P("ctx", None, "head"),
        ),
        check_vma=False,
    )
```

profile of v0, /device:TPU:0, one launch (start us, length us, event | category | flops | bytes accessed | tf_op | source)
XLA Modules:
  0.0 211.3 jit_solution(12901582267295648135)
XLA Ops:
  8.2 2.3 %reduce-window.6 = s32[8,8,128]{2,1,0:T(8,128)S(1)} reduce-window(s32[8,8,128]{2,1,0:T(8,128)S(1)} %fusion.27, s32[]{:T(128)} %constant.5.clone.1), window={size=1x1x128 pad=0_0x0_0x127_0}, to_apply=%region_0.0 | reduce-window | flops 1040384 | bytes 65540 | tf_op jit(solution)/shard_map/reduce-window
  12.7 2.7 %fusion.2 = f32[48,14336]{1,0:T(8,128)S(1)} fusion(bf16[128,7168]{1,0:T(8,128)(2,1)} %param.13, bf16[128,7168]{1,0:T(8,128)(2,1)} %param.7, bf16[128,48]{0,1:T(8,128)(2,1)S(1)} %get-tuple-element.8), kind=kOutput, calls=%fused_computation.9 | convolution fusion | flops 183500800 | bytes 6434816 | tf_op jit(solution)/shard_map/dot_general | solution.py:47
  16.8 2.1 %copy.69 = bf16[8,4,6,1792]{3,2,1,0:T(8,128)(2,1)} copy(bf16[8,4,6,1792]{3,1,2,0:T(4,128)(2,1)} %bitcast.71) | data formatting | bytes 1376256 | tf_op jit(solution)/shard_map/reshape | solution.py:74
  19.0 7.4 %all-to-all-start.1 = ((bf16[32,6,1792]{2,1,0:T(8,128)(2,1)}), bf16[32,6,1792]{2,1,0:T(8,128)(2,1)}, u32[]{:S(2)}, u32[]{:S(2)}) async-start(bf16[32,6,1792]{2,1,0:T(8,128)(2,1)} %bitcast.69), calls=%async_computation.1 | async-start | bytes 1835008 | tf_op jit(solution)/shard_map/all_to_all | solution.py:73
  27.3 1.9 reshape.100
  30.2 19.6 %all-to-all-done.1 = bf16[32,6,1792]{2,1,0:T(8,128)(2,1)} async-done(((bf16[32,6,1792]{2,1,0:T(8,128)(2,1)}), bf16[32,6,1792]{2,1,0:T(8,128)(2,1)}, u32[]{:S(2)}, u32[]{:S(2)}) %all-to-all-start.1) | async-done | bytes 688160 | tf_op jit(solution)/shard_map/all_to_all | solution.py:73
  49.8 3.7 %all-to-all-start = ((bf16[32,6,1792]{2,1,0:T(8,128)(2,1)}), bf16[32,6,1792]{2,1,0:T(8,128)(2,1)}, u32[]{:S(2)}, u32[]{:S(2)}) async-start(bf16[32,6,1792]{2,1,0:T(8,128)(2,1)} %bitcast.68), calls=%async_computation | async-start | bytes 1835008 | tf_op jit(solution)/shard_map/all_to_all | solution.py:66
  55.0 4.5 %fusion.8 = f32[192,1024]{1,0:T(8,128)} fusion(bf16[192,1792]{1,0:T(8,128)(2,1)S(1)} %reshape.105, bf16[1,1024,1792]{2,1,0:T(8,128)(2,1)} %param.12), kind=kOutput, calls=%fused_computation.15 | convolution fusion | flops 704643072 | bytes 5144576 | tf_op jit(solution)/shard_map/dot_general | solution.py:88
  59.5 17.5 %all-to-all-done = bf16[32,6,1792]{2,1,0:T(8,128)(2,1)} async-done(((bf16[32,6,1792]{2,1,0:T(8,128)(2,1)}), bf16[32,6,1792]{2,1,0:T(8,128)(2,1)}, u32[]{:S(2)}, u32[]{:S(2)}) %all-to-all-start) | async-done | bytes 688160 | tf_op jit(solution)/shard_map/all_to_all | solution.py:66
  78.4 4.8 %fusion.1 = f32[192,2048]{1,0:T(8,128)S(1)} fusion(bf16[192,1792]{1,0:T(8,128)(2,1)S(1)} %reshape.102, bf16[1792,1024]{1,0:T(8,128)(2,1)} %bitcast.76, bf16[1792,1024]{1,0:T(8,128)(2,1)} %bitcast.78), kind=kOutput, calls=%fused_computation.5 | convolution fusion | flops 1423966208 | bytes 9601024 | tf_op jit(solution)/shard_map/dot_general | solution.py:87
  84.9 32.2 %reduce-scatter.2.cloned.1.call-done = f32[48,3072]{1,0:T(8,128)} async-done(((f32[192,3072]{1,0:T(8,128)}), f32[48,3072]{1,0:T(8,128)}) %reduce-scatter.2.cloned.1.call-update) | async-done | bytes 589840 | tf_op jit(solution)/shard_map/reduce_scatter | solution.py:91
  119.1 17.7 %all-gather.2.cloned.1.call-done = bf16[192,3072]{1,0:T(8,128)(2,1)} async-done(((bf16[48,3072]{1,0:T(8,128)(2,1)}), bf16[192,3072]{1,0:T(8,128)(2,1)}) %all-gather.2.cloned.1.call-update) | async-done | bytes 1179664 | tf_op jit(solution)/shard_map/all_gather | solution.py:94
  136.8 3.9 %fusion.12 = bf16[192,1792]{1,0:T(8,128)(2,1)} fusion(bf16[1,1024,1792]{2,1,0:T(8,128)(2,1)} %param.12, bf16[192,3072]{1,0:T(8,128)(2,1)} %all-gather.2.cloned.1.call-done), kind=kOutput, calls=%fused_computation.19 | convolution fusion | flops 704987136 | bytes 4751360 | tf_op jit(solution)/shard_map/dot_general | solution.py:97
  140.7 2.1 %reshape.106 = bf16[32,6,1792]{2,1,0:T(8,128)(2,1)} reshape(bf16[192,1792]{1,0:T(8,128)(2,1)} %fusion.12) | data formatting | bytes 1376256 | tf_op jit(solution)/shard_map/reshape | solution.py:113
  142.8 4.7 %all-to-all-start.2 = ((bf16[32,6,1792]{2,1,0:T(8,128)(2,1)}), bf16[32,6,1792]{2,1,0:T(8,128)(2,1)}, u32[]{:S(2)}, u32[]{:S(2)}) async-start(bf16[32,6,1792]{2,1,0:T(8,128)(2,1)} %reshape.106), calls=%async_computation.3 | async-start | bytes 1835008 | tf_op jit(solution)/shard_map/all_to_all | solution.py:112
  147.6 6.8 %fusion.11 = bf16[192,1792]{1,0:T(8,128)(2,1)} fusion(bf16[1792,1024]{1,0:T(8,128)(2,1)} %bitcast.77, bf16[1792,1024]{1,0:T(8,128)(2,1)} %bitcast.79, bf16[192,3072]{1,0:T(8,128)(2,1)} %all-gather.2.cloned.1.call-done), kind=kOutput, calls=%fused_computation.18 | convolution fusion | flops 1424310272 | bytes 8814592 | tf_op jit(solution)/shard_map/dot_general | solution.py:108
  154.4 2.1 %reshape.109 = bf16[32,6,1792]{2,1,0:T(8,128)(2,1)} reshape(bf16[192,1792]{1,0:T(8,128)(2,1)} %fusion.11) | data formatting | bytes 1376256 | tf_op jit(solution)/shard_map/reshape | solution.py:120
  156.5 6.2 %convolution_convert_fusion.2 = bf16[1792,2048]{1,0:T(8,128)(2,1)} fusion(bf16[192,1792]{1,0:T(8,128)(2,1)S(1)} %reshape.102, bf16[192,3072]{1,0:T(8,128)(2,1)} %all-gather.2.cloned.1.call-done), kind=kOutput, calls=%fused_computation.2 | convolution fusion | flops 1412956160 | bytes 8814592 | tf_op jit(solution)/shard_map/dot_general | solution.py:103
  162.7 8.2 %all-to-all-done.2 = bf16[32,6,1792]{2,1,0:T(8,128)(2,1)} async-done(((bf16[32,6,1792]{2,1,0:T(8,128)(2,1)}), bf16[32,6,1792]{2,1,0:T(8,128)(2,1)}, u32[]{:S(2)}, u32[]{:S(2)}) %all-to-all-start.2) | async-done | bytes 688160 | tf_op jit(solution)/shard_map/all_to_all | solution.py:112
  171.0 3.9 %all-to-all-start.3 = ((bf16[32,6,1792]{2,1,0:T(8,128)(2,1)}), bf16[32,6,1792]{2,1,0:T(8,128)(2,1)}, u32[]{:S(2)}, u32[]{:S(2)}) async-start(bf16[32,6,1792]{2,1,0:T(8,128)(2,1)} %reshape.109), calls=%async_computation.4 | async-start | bytes 1835008 | tf_op jit(solution)/shard_map/all_to_all | solution.py:119
  174.9 4.2 %fusion.10 = bf16[1,1024,1792]{2,1,0:T(8,128)(2,1)} fusion(bf16[192,1792]{1,0:T(8,128)(2,1)} %copy-done.1, bf16[192,3072]{1,0:T(8,128)(2,1)} %all-gather.2.cloned.1.call-done), kind=kOutput, calls=%fused_computation.17 | convolution fusion | flops 706478080 | bytes 4751360 | tf_op jit(solution)/shard_map/dot_general | solution.py:100
  179.1 7.0 %slice_bitcast_fusion = (bf16[1,1792,1024]{2,1,0:T(8,128)(2,1)}, bf16[1,1792,1024]{2,1,0:T(8,128)(2,1)}) fusion(bf16[1792,2048]{1,0:T(8,128)(2,1)} %convolution_convert_fusion.2), kind=kLoop, calls=%fused_computation.7 | loop fusion | bytes 14680064 | tf_op jit(solution)/shard_map/broadcast_in_dim | solution.py:139
  188.7 9.4 %all-to-all-done.3 = bf16[32,6,1792]{2,1,0:T(8,128)(2,1)} async-done(((bf16[32,6,1792]{2,1,0:T(8,128)(2,1)}), bf16[32,6,1792]{2,1,0:T(8,128)(2,1)}, u32[]{:S(2)}, u32[]{:S(2)}) %all-to-all-start.3) | async-done | bytes 688160 | tf_op jit(solution)/shard_map/all_to_all | solution.py:119
  201.6 2.9 %convolution_convert_fusion.1 = bf16[128,7168]{1,0:T(8,128)(2,1)} fusion(f32[128,48]{0,1:T(8,128)S(1)} %get-tuple-element.7, bf16[48,7168]{1,0:T(8,128)(2,1)S(1)} %bitcast.67), kind=kOutput, calls=%fused_computation.1 | convolution fusion | flops 529399808 | bytes 2547712 | tf_op jit(solution)/shard_map/dot_general | solution.py:129
  (36 shorter events, 19.0 us)
Async XLA Ops:
  19.0 30.8 %all-to-all-start.1 = ((bf16[32,6,1792]{2,1,0:T(8,128)(2,1)}), bf16[32,6,1792]{2,1,0:T(8,128)(2,1)}, u32[]{:S(2)}, u32[]{:S(2)}) async-start(bf16[32,6,1792]{2,1,0:T(8,128)(2,1)} %bitcast.69), calls=%async_computation.1 | async-start | bytes 1835008 | tf_op jit(solution)/shard_map/all_to_all | solution.py:73
  49.8 27.2 %all-to-all-start = ((bf16[32,6,1792]{2,1,0:T(8,128)(2,1)}), bf16[32,6,1792]{2,1,0:T(8,128)(2,1)}, u32[]{:S(2)}, u32[]{:S(2)}) async-start(bf16[32,6,1792]{2,1,0:T(8,128)(2,1)} %bitcast.68), calls=%async_computation | async-start | bytes 1835008 | tf_op jit(solution)/shard_map/all_to_all | solution.py:66
  53.6 63.5 %reduce-scatter.2.cloned.1.call-start = ((), (), s32[]{:S(2)}) async-start(), calls=%async_computation.5 | async-start | bytes 2949120 | tf_op jit(solution)/shard_map/reduce_scatter | solution.py:91
  55.0 4.5 %copy-start.1 = (bf16[192,1792]{1,0:T(8,128)(2,1)}, bf16[192,1792]{1,0:T(8,128)(2,1)S(1)}, u32[]{:S(2)}) copy-start(bf16[192,1792]{1,0:T(8,128)(2,1)S(1)} %reshape.105) | copy-start | bytes 2064388
  78.4 4.8 %copy-start = (f32[192,1024]{1,0:T(8,128)S(1)}, f32[192,1024]{1,0:T(8,128)}, u32[]{:S(2)}) copy-start(f32[192,1024]{1,0:T(8,128)} %fusion.8) | copy-start | bytes 2359300
  84.9 51.9 %all-gather.2.cloned.1.call-start = ((), (), s32[]{:S(2)}) async-start(), calls=%async_computation.6 | async-start | bytes 1474560 | tf_op jit(solution)/shard_map/all_gather | solution.py:94
  142.8 28.1 %all-to-all-start.2 = ((bf16[32,6,1792]{2,1,0:T(8,128)(2,1)}), bf16[32,6,1792]{2,1,0:T(8,128)(2,1)}, u32[]{:S(2)}, u32[]{:S(2)}) async-start(bf16[32,6,1792]{2,1,0:T(8,128)(2,1)} %reshape.106), calls=%async_computation.3 | async-start | bytes 1835008 | tf_op jit(solution)/shard_map/all_to_all | solution.py:112
  171.0 27.2 %all-to-all-start.3 = ((bf16[32,6,1792]{2,1,0:T(8,128)(2,1)}), bf16[32,6,1792]{2,1,0:T(8,128)(2,1)}, u32[]{:S(2)}, u32[]{:S(2)}) async-start(bf16[32,6,1792]{2,1,0:T(8,128)(2,1)} %reshape.109), calls=%async_computation.4 | async-start | bytes 1835008 | tf_op jit(solution)/shard_map/all_to_all | solution.py:119
Sparse Core Ops, SparseCore 0:
  85.0 32.0 reduce-scatter.1
  119.3 17.4 all-gather.1
where the time goes:
time: 212 us; the launch traced here: 211 us
  waiting for transfers between devices  105 us (50%)
  matrix products  38.7 us (18%)
  local copies, waits for them, and re-layouts  25.8 us (12%)
  starting transfers between devices  19.9 us (9%)
  between operations  14.2 us (7%)
  other arithmetic  8.07 us (4%)
    reduce_scatter x1, waiting for transfers between devices, on_device(): lax.psum_scatter(jnp.concatenate([forward, backward], axis=1), 'head', sc...  32.2 us
    all_to_all x1, waiting for transfers between devices, on_device(): lax.all_to_all(to_slices(do_rows).reshape(experts * groups, CAP, slice_wi...  19.6 us
    all_gather x1, waiting for transfers between devices, on_device(): lax.all_gather(activate(row_share, hidden_width), 'head', axis=0, tiled=T...  17.7 us
    all_to_all x1, waiting for transfers between devices, on_device(): lax.all_to_all(to_slices(x_rows).reshape(experts * groups, CAP, slice_wid...  17.5 us
    all_to_all x1, waiting for transfers between devices, on_device(): lax.all_to_all(grad_rows.reshape(experts * groups, CAP, slice_width), ('c...  9.44 us
    all_to_all x1, waiting for transfers between devices, on_device(): lax.all_to_all(expert_out.reshape(experts * groups, CAP, slice_width), ('...  8.25 us
    all_to_all x1, starting transfers between devices, on_device(): lax.all_to_all(to_slices(do_rows).reshape(experts * groups, CAP, slice_wi...  7.41 us
    broadcast_in_dim x1, local copies, waits for them, and re-layouts, on_device(): grad_up[None]  7.04 us
  transfers between devices with their start and end apart: 6, of which 6 were waited for; matrix products, arithmetic and copies ran while one was open for 18% of the time, Pallas kernels for 0%

commit v1 on v0

v1 whole, which is shorter than its diff:
```python
import functools

import jax
import jax.numpy as jnp
from jax import lax
from jax.experimental import pallas as pl
from jax.experimental.pallas import tpu as pltpu
from jax.sharding import PartitionSpec as P

CAP = 6
PARTS = 2
SLOTS = CAP // PARTS
ROWS = 16
LANES = 128
MESH = pl.DeviceIdType.MESH
F32 = jnp.float32
BF16 = jnp.bfloat16
VMEM_BYTES = 60 * 1024 * 1024


def block_cols(slice_width):
    tiles = slice_width // LANES
    cols = -(-2 * SLOTS * tiles // ROWS)
    rest = tiles - 2 * cols
    assert 0 <= 2 * rest <= cols
    return cols, rest


def dot(a, b):
    return jnp.dot(a, b, preferred_element_type=F32)


def dot_nt(a, b):
    return lax.dot_general(a, b, (((1,), (1,)), ((), ())), preferred_element_type=F32)


def dot_tn(a, b):
    return lax.dot_general(a, b, (((0,), (0,)), ((), ())), preferred_element_type=F32)


def iota(shape, dim):
    return lax.broadcasted_iota(jnp.int32, shape, dim)


def tile_cols(value, start, count):
    return value[:, start * LANES : (start + count) * LANES]


def slot_in_part(i):
    return jnp.where(
        i < 3, i, jnp.where(i < 6, i - 3, jnp.where(i < 9, i - 6, jnp.where(i < 12, i - 9, i - 12)))
    )


def exchange_kernel(
    experts, heads,
    tok_ref, dy_ref, routes_ref, weight_ref, gate_hbm, up_hbm, down_hbm,
    x_ref, d_ref, act_ref, back_ref,
    gate_w, up_w, down_w, turn, send1, recv1, send2, pair_send, pair_recv, y_send, y_recv,
    w_sem, own_sem, s1_sem, r1_sem, s2_sem, r2_sem, ps_sem, pr_sem, ys_sem, yr_sem, as_sem, ar_sem,
):
    total = experts * heads
    cores, y_size = 2, heads // 2
    ctx, head = lax.axis_index("ctx"), lax.axis_index("head")
    me = ctx * heads + head
    core, y = head % cores, head // cores
    toks = tok_ref.shape[0]
    picks = routes_ref.shape[1]
    slice_width, hidden = gate_w.shape
    half = hidden // 2
    cols, rest = block_cols(slice_width)
    part_rows = total * SLOTS
    group_rows = 16 * SLOTS
    sibling = {"ctx": ctx, "head": y * cores + 1 - core}

    weight_copies = [
        pltpu.make_async_copy(src, dst, w_sem.at[n])
        for n, (src, dst) in enumerate(((gate_hbm, gate_w), (up_hbm, up_w), (down_hbm, down_w)))
    ]
    for copy in weight_copies:
        copy.start()

    barrier = pltpu.get_barrier_semaphore()

    def greet(step, carry):
        j = (me + step) % total
        pl.semaphore_signal(
            barrier, inc=1, device_id={"ctx": j // heads, "head": j % heads}, device_id_type=MESH
        )
        return carry

    lax.fori_loop(1, total, greet, 0)

    turn[...] = jnp.zeros_like(turn)
    turn[:, :picks] = routes_ref[...].astype(F32)
    routes_t = turn[...].T[:picks]
    turn[:, :picks] = weight_ref[...]
    weight_t = turn[...].T[:picks]
    out_rows = experts * ROWS
    row = iota((out_rows, 1), 0)
    row_expert = (row // ROWS).astype(F32)
    i = row % ROWS
    hit = jnp.zeros((out_rows, toks), F32)
    pick_weight = jnp.zeros((out_rows, toks), F32)
    for k in range(picks):
        same = routes_t[k : k + 1] == row_expert
        hit = jnp.where(same, 1.0, hit)
        pick_weight = jnp.where(same, weight_t[k : k + 1], pick_weight)
    earlier = (iota((toks, toks), 0) < iota((toks, toks), 1)).astype(BF16)
    position = dot(hit.astype(BF16), earlier)

    def fill(part):
        want = (slot_in_part(i) + part * SLOTS).astype(F32)
        chosen = jnp.where((position == want) & (i < 15), hit, 0.0)
        slot_weight = jnp.sum(chosen * pick_weight, axis=1, keepdims=True)
        picked, scale = [], []
        for kind in range(2):
            second = ((i >= 3) & (i < 6)) | ((i >= 9) & (i < 12))
            if kind:
                second = second | (i >= 12)
            picked.append(
                jnp.concatenate(
                    [jnp.where(second, 0.0, chosen), jnp.where(second, chosen, 0.0)], axis=1
                ).astype(BF16)
            )
            scale.append(jnp.where(second, slot_weight, 1.0))
        for h in range(heads):
            width = pl.ds(h * slice_width, slice_width)
            source = jnp.concatenate([tok_ref[:, width], dy_ref[:, width]], axis=0)
            full = dot(picked[0], source) * scale[0]
            tail = dot(picked[1], tile_cols(source, 2 * cols, rest)) * scale[1]
            for j in range(cols):
                value = jnp.where(i < 6, tile_cols(full, j, 1), tile_cols(full, cols + j, 1))
                if j < 2 * rest:
                    last = tile_cols(tail, j // 2, 1) if j % 2 else tile_cols(full, 2 * cols + j // 2, 1)
                    value = jnp.where(i < 12, value, last)
                send1[part, h, :, :, j * LANES : (j + 1) * LANES] = value.astype(BF16).reshape(
                    experts, ROWS, LANES
                )

    def ship(part):
        pltpu.make_async_copy(
            send1.at[part, head, ctx], recv1.at[part, me], own_sem.at[part]
        ).start()

        def one(step, carry):
            j = (me + step) % total
            e, h = j // heads, j % heads
            pltpu.make_async_remote_copy(
                src_ref=send1.at[part, h, e],
                dst_ref=recv1.at[part, me],
                send_sem=s1_sem.at[part],
                recv_sem=r1_sem.at[part],
                device_id={"ctx": e, "head": h},
                device_id_type=MESH,
            ).start()
            return carry

        lax.fori_loop(1, total, one, 0)

    def wait_blocks(part, sem):
        blocks = recv1.at[part, pl.ds(0, total - 1)]
        pltpu.make_async_copy(blocks, blocks, sem.at[part]).wait()

    fill(0)
    pl.semaphore_wait(barrier, total - 1)
    ship(0)
    for part in range(1, PARTS):
        fill(part)
        ship(part)
    for copy in weight_copies:
        copy.wait()

    def places(first, rows_out):
        out, col = iota((rows_out, 16 * ROWS), 0), iota((rows_out, 16 * ROWS), 1)
        kind = (out >= group_rows).astype(jnp.int32)
        slot = out - kind * group_rows
        return (col == (slot // 3) * ROWS + slot % 3 + kind * 3 + first).astype(BF16)

    place = [places(0, 2 * group_rows), places(6, 2 * group_rows), places(12, group_rows)]

    def activate(part, sums):
        gate, up, back = sums[:, :half], sums[:, half : 2 * half], sums[:, 2 * half :]
        sig = jax.nn.sigmoid(gate)
        smooth = gate * sig
        slope = sig * (1.0 + gate * (1.0 - sig))
        act_ref[part, core, :, :half] = (smooth * up).astype(BF16)
        act_ref[part, core, :, half : 2 * half] = (back * up * slope).astype(BF16)
        act_ref[part, core, :, 2 * half :] = (back * smooth).astype(BF16)

    def project(x, d, side):
        units = pl.ds(pl.multiple_of(side * half, half), half)
        return dot(x, gate_w[:, units]), dot(x, up_w[:, units]), dot_nt(d, down_w[units, :])

    def work(part, carry):
        pltpu.make_async_copy(
            send1.at[part, head, ctx], recv1.at[part, me], own_sem.at[part]
        ).wait()
        wait_blocks(part, r1_sem)
        for g in range(total // 16):
            block = recv1[part, pl.ds(g * 16, 16)].reshape(16 * ROWS, cols * LANES)
            at = pl.ds(pl.multiple_of(part * part_rows + g * group_rows, 16), group_rows)
            for band in range(2):
                value = dot(place[band], block).astype(BF16)
                span = pl.ds(band * cols * LANES, cols * LANES)
                x_ref[at, span] = value[:group_rows]
                d_ref[at, span] = value[group_rows:]
            tail = dot(place[2], tile_cols(block, 0, 2 * rest)).astype(BF16)
            for q in range(rest):
                span = pl.ds((2 * cols + q) * LANES, LANES)
                x_ref[at, span] = tile_cols(tail, 2 * q, 1)
                d_ref[at, span] = tile_cols(tail, 2 * q + 1, 1)

        at = pl.ds(pl.multiple_of(part * part_rows, 16), part_rows)
        x, d = x_ref[at, :], d_ref[at, :]
        for n, value in enumerate(project(x, d, 1 - core)):
            pair_send[part, :, n * half : (n + 1) * half] = value
        to_pair = pltpu.make_async_remote_copy(
            src_ref=pair_send.at[part],
            dst_ref=pair_recv.at[part],
            send_sem=ps_sem.at[part],
            recv_sem=pr_sem.at[part],
            device_id=sibling,
            device_id_type=MESH,
        )
        to_pair.start()
        mine = jnp.concatenate(project(x, d, core), axis=1)
        to_pair.wait_recv()
        mine = mine + pair_recv[part]
        y_send[part] = mine.astype(BF16)
        to_y = []
        for q in range(1, y_size):
            to_y.append(
                pltpu.make_async_remote_copy(
                    src_ref=y_send.at[part],
                    dst_ref=y_recv.at[part, q - 1],
                    send_sem=ys_sem.at[part, q - 1],
                    recv_sem=yr_sem.at[part, q - 1],
                    device_id={"ctx": ctx, "head": ((y + q) % y_size) * cores + core},
                    device_id_type=MESH,
                )
            )
            to_y[-1].start()
        for q, copy in enumerate(to_y):
            copy.wait_recv()
            mine = mine + y_recv[part, q].astype(F32)
        activate(part, mine)
        act_copy = pltpu.make_async_remote_copy(
            src_ref=act_ref.at[part, core],
            dst_ref=act_ref.at[part, core],
            send_sem=as_sem.at[part],
            recv_sem=ar_sem.at[part],
            device_id=sibling,
            device_id_type=MESH,
        )
        act_copy.start()
        act_copy.wait_recv()

        out, grad = 0.0, 0.0
        for side in range(2):
            units = pl.ds(side * half, half)
            out += dot(act_ref[part, side, :, :half], down_w[units, :])
            grad += dot_nt(act_ref[part, side, :, half : 2 * half], gate_w[:, units])
            grad += dot_nt(act_ref[part, side, :, 2 * half :], up_w[:, units])
        out, grad = out.astype(BF16), grad.astype(BF16)
        for g in range(total // 16):
            rows = slice(g * group_rows, (g + 1) * group_rows)
            both = jnp.concatenate([out[rows], grad[rows]], axis=0)
            block = dot_tn(place[0], tile_cols(both, 0, cols)) + dot_tn(
                place[1], tile_cols(both, cols, cols)
            )
            tail = []
            for q in range(rest):
                tail += [tile_cols(v, 2 * cols + q, 1) for v in (out[rows], grad[rows])]
            tail = dot_tn(place[2], jnp.concatenate(tail, axis=1))
            span = 2 * rest * LANES
            block = block.reshape(16, ROWS, cols * LANES)
            send2[part, pl.ds(g * 16, 16), :, :span] = (
                block[:, :, :span] + tail.reshape(16, ROWS, span)
            ).astype(BF16)
            if span < cols * LANES:
                send2[part, pl.ds(g * 16, 16), :, span:] = block[:, :, span:].astype(BF16)

        pltpu.make_async_copy(
            send2.at[part, me], back_ref.at[part, me], own_sem.at[PARTS + part]
        ).start()

        def one(step, inner):
            j = (me + step) % total
            pltpu.make_async_remote_copy(
                src_ref=send2.at[part, j],
                dst_ref=back_ref.at[part, me],
                send_sem=s2_sem.at[part],
                recv_sem=r2_sem.at[part],
                device_id={"ctx": j // heads, "head": j % heads},
                device_id_type=MESH,
            ).start()
            return inner

        lax.fori_loop(1, total, one, 0)
        to_pair.wait_send()
        for copy in to_y:
            copy.wait_send()
        act_copy.wait_send()
        return carry

    lax.fori_loop(0, PARTS, work, 0)

    for part in range(PARTS):
        wait_blocks(part, s1_sem)
        wait_blocks(part, s2_sem)
        pltpu.make_async_copy(
            send2.at[part, me], back_ref.at[part, me], own_sem.at[PARTS + part]
        ).wait()
        wait_blocks(part, r2_sem)


def finish_kernel(
    experts, heads,
    routes_ref, weight_ref, dy_ref, back_ref, x_ref, d_ref, act_ref,
    moe_ref, grad_tok_ref, grad_route_ref, gate_ref, up_ref, down_ref,
    weighted, plain, inner,
):
    step = pl.program_id(0)
    toks, picks = routes_ref.shape
    slice_width = dy_ref.shape[1]
    cols, rest = block_cols(slice_width)
    width = experts * ROWS
    half = act_ref.shape[3] // 3
    lane = iota((1, width), 1)
    lane_expert = lane // ROWS
    i = lane % ROWS

    @pl.when(step == 0)
    def _():
        hit = jnp.zeros((toks, width), F32)
        pick_weight = jnp.zeros((toks, width), F32)
        for k in range(picks):
            same = routes_ref[:, k : k + 1] == lane_expert
            hit = jnp.where(same, 1.0, hit)
            pick_weight = jnp.where(same, weight_ref[:, k : k + 1], pick_weight)
        earlier = (iota((toks, toks), 0) > iota((toks, toks), 1)).astype(BF16)
        position = dot(earlier, hit.astype(BF16))
        for part in range(PARTS):
            want = (slot_in_part(i) + part * SLOTS).astype(F32)
            chosen = jnp.where((position == want) & (i < 15), hit, 0.0)
            scaled = chosen * pick_weight
            high = scaled.astype(BF16)
            low = (scaled - high.astype(F32)).astype(BF16)
            for band in range(3):
                first = (i >= 6 * band) & (i < 6 * band + 3)
                second = first if band == 2 else (i >= 6 * band + 3) & (i < 6 * band + 6)
                zero = jnp.zeros((), BF16)
                weighted[part, band, :, :width] = jnp.where(first, high, zero)
                weighted[part, band, :, width:] = jnp.where(first, low, zero)
                plain[band, :, part * width : (part + 1) * width] = jnp.where(
                    second, chosen, 0.0
                ).astype(BF16)
        inner[...] = jnp.zeros_like(inner)

    blocks = [back_ref[part, :, 0].reshape(width, cols * LANES) for part in range(PARTS)]
    odd = [jnp.concatenate([tile_cols(b, 2 * q + 1, 1) for q in range(rest)], axis=1) for b in blocks]
    even = [jnp.concatenate([tile_cols(b, 2 * q, 1) for q in range(rest)], axis=1) for b in blocks]
    for band, firsts, seconds, start, count in (
        (0, blocks, blocks, 0, cols),
        (1, blocks, blocks, cols, cols),
        (2, even, odd, 2 * cols, rest),
    ):
        span = slice(start * LANES, (start + count) * LANES)
        moe = 0.0
        for part in range(PARTS):
            moe += dot(weighted[part, band], jnp.concatenate([firsts[part]] * 2, axis=0))
            inner[part, band] += dot_nt(dy_ref[:, span], firsts[part])
        moe_ref[:, span] = moe.astype(BF16)
        grad_tok_ref[:, span] = dot(plain[band], jnp.concatenate(seconds, axis=0)).astype(BF16)

    @pl.when(step == pl.num_programs(0) - 1)
    def _():
        found = 0.0
        for part in range(PARTS):
            for band in range(3):
                chosen = weighted[part, band, :, :width].astype(F32) > 0.0
                found += jnp.where(chosen, inner[part, band], 0.0)
        for k in range(picks):
            grad_route_ref[:, k : k + 1] = jnp.sum(
                jnp.where(routes_ref[:, k : k + 1] == lane_expert, found, 0.0), axis=1, keepdims=True
            )

    count = down_ref.shape[0]
    side_steps = half // count
    offset = (step % side_steps) * count

    def units(start):
        at = pl.ds(pl.multiple_of(start * half + offset, count), count)
        return jnp.concatenate(
            [act_ref[part, step // side_steps, :, at] for part in range(PARTS)], axis=0
        )

    gate_ref[...] = dot_tn(x_ref[...], units(1)).astype(BF16)
    up_ref[...] = dot_tn(x_ref[...], units(2)).astype(BF16)
    down_ref[...] = dot_tn(units(0), d_ref[...]).astype(BF16)


def on_device(tokens, routes, route_weight, w_gate, w_up, w_down, grad_out):
    experts = lax.axis_size("ctx")
    heads = lax.axis_size("head")
    total = experts * heads
    toks, model_width = tokens.shape
    picks = routes.shape[1]
    slice_width, hidden = w_gate.shape[1:]
    half = hidden // 2
    cols, rest = block_cols(slice_width)
    part_rows = total * SLOTS
    all_rows = PARTS * part_rows
    y_others = max(1, heads // 2 - 1)
    vmem = pl.BlockSpec(memory_space=pltpu.VMEM)
    hbm = pl.BlockSpec(memory_space=pl.ANY)
    block = (ROWS, cols * LANES)
    dma = pltpu.SemaphoreType.DMA
    x_rows, d_rows, acts, back = pl.pallas_call(
        functools.partial(exchange_kernel, experts, heads),
        out_shape=(
            jax.ShapeDtypeStruct((all_rows, slice_width), BF16),
            jax.ShapeDtypeStruct((all_rows, slice_width), BF16),
            jax.ShapeDtypeStruct((PARTS, 2, part_rows, 3 * half), BF16),
            jax.ShapeDtypeStruct((PARTS, total) + block, BF16),
        ),
        in_specs=[vmem] * 4 + [hbm] * 3,
        out_specs=(vmem,) * 4,
        scratch_shapes=[
            pltpu.VMEM((slice_width, hidden), BF16),
            pltpu.VMEM((slice_width, hidden), BF16),
            pltpu.VMEM((hidden, slice_width), BF16),
            pltpu.VMEM((toks, LANES), F32),
            pltpu.VMEM((PARTS, heads, experts) + block, BF16),
            pltpu.VMEM((PARTS, total) + block, BF16),
            pltpu.VMEM((PARTS, total) + block, BF16),
            pltpu.VMEM((PARTS, part_rows, 3 * half), F32),
            pltpu.VMEM((PARTS, part_rows, 3 * half), F32),
            pltpu.VMEM((PARTS, part_rows, 3 * half), BF16),
            pltpu.VMEM((PARTS, y_others, part_rows, 3 * half), BF16),
            dma((3,)),
            dma((2 * PARTS,)),
            dma((PARTS,)),
            dma((PARTS,)),
            dma((PARTS,)),
            dma((PARTS,)),
            dma((PARTS,)),
            dma((PARTS,)),
            dma((PARTS, y_others)),
            dma((PARTS, y_others)),
            dma((PARTS,)),
            dma((PARTS,)),
        ],
        compiler_params=pltpu.CompilerParams(
            collective_id=0, has_side_effects=True, vmem_limit_bytes=VMEM_BYTES
        ),
    )(tokens, grad_out, routes, route_weight, w_gate[0], w_up[0], w_down[0])

    back = back.reshape((PARTS, experts, heads) + block)

    def whole(shape):
        return pl.BlockSpec(shape, lambda h: (0,) * len(shape))

    units = hidden // heads
    moe_out, grad_tokens, grad_route, grad_gate, grad_up, grad_down = pl.pallas_call(
        functools.partial(finish_kernel, experts, heads),
        grid=(heads,),
        in_specs=[
            whole((toks, picks)),
            whole((toks, picks)),
            pl.BlockSpec((toks, slice_width), lambda h: (0, h)),
            pl.BlockSpec((PARTS, experts, 1) + block, lambda h: (0, 0, h, 0, 0)),
            whole((all_rows, slice_width)),
            whole((all_rows, slice_width)),
            whole((PARTS, 2, part_rows, 3 * half)),
        ],
        out_specs=(
            pl.BlockSpec((toks, slice_width), lambda h: (0, h)),
            pl.BlockSpec((toks, slice_width), lambda h: (0, h)),
            whole((toks, picks)),
            pl.BlockSpec((slice_width, units), lambda h: (0, h)),
            pl.BlockSpec((slice_width, units), lambda h: (0, h)),
            pl.BlockSpec((units, slice_width), lambda h: (h, 0)),
        ),
        out_shape=(
            jax.ShapeDtypeStruct((toks, model_width), BF16),
            jax.ShapeDtypeStruct((toks, model_width), BF16),
            jax.ShapeDtypeStruct((toks, picks), F32),
            jax.ShapeDtypeStruct((slice_width, hidden), BF16),
            jax.ShapeDtypeStruct((slice_width, hidden), BF16),
            jax.ShapeDtypeStruct((hidden, slice_width), BF16),
        ),
        scratch_shapes=[
            pltpu.VMEM((PARTS, 3, toks, 2 * experts * ROWS), BF16),
            pltpu.VMEM((3, toks, PARTS * experts * ROWS), BF16),
            pltpu.VMEM((PARTS, 3, toks, experts * ROWS), F32),
        ],
        compiler_params=pltpu.CompilerParams(vmem_limit_bytes=VMEM_BYTES),
    )(routes, route_weight, grad_out, back, x_rows, d_rows, acts)
    return (moe_out, grad_tokens, grad_route, grad_gate[None], grad_up[None], grad_down[None])


def solution(mesh):
    tok = P(("ctx", "head"), None)
    col, row = P("ctx", "head", None), P("ctx", None, "head")
    return jax.shard_map(
        on_device,
        mesh=mesh,
        in_specs=(tok, tok, tok, col, col, row, tok),
        out_specs=(tok, tok, tok, col, col, row),
        check_vma=False,
    )
```

time: 212 us -> 106 us (0.50)
  the two profiles are of different devices: /device:TPU:0 before, /device:TPU:27 now
where the time goes in v1:
time: 106 us
  Pallas kernels  101 us (95%)
  local copies, waits for them, and re-layouts  4.32 us (4%)
    pallas_call x1, Pallas kernels, on_device(): pl.pallas_call(functools.partial(exchange_kernel, experts, heads), out_sh...  89.3 us
    pallas_call x1, Pallas kernels, on_device(): pl.pallas_call(functools.partial(finish_kernel, experts, heads), grid=(he...  11.9 us
    unnamed x3, local copies, waits for them, and re-layouts  4.32 us

profile of v1, /device:TPU:27, one launch (start us, length us, event | category | flops | bytes accessed | tf_op | source)
XLA Modules:
  0.0 106.2 jit_solution(5380088779949097533)
XLA Ops:
  0.6 1.4 %copy.15.routes_ref = s32[128,8]{1,0:T(8,128)} copy(s32[128,8]{0,1:T(8,128)} %param.8) | data formatting | bytes 8192 | tf_op args[1]
  2.0 1.4 %copy.16.weight_ref = f32[128,8]{1,0:T(8,128)} copy(f32[128,8]{0,1:T(8,128)} %param.9) | data formatting | bytes 8192 | tf_op args[2]
  3.5 89.3 %shard_map.118 = (bf16[192,1792]{1,0:T(8,128)(2,1)}, bf16[192,1792]{1,0:T(8,128)(2,1)}, bf16[2,2,96,1536]{3,2,1,0:T(8,128)(2,1)}, bf16[2,32,16,768]{3,2,1,0:T(8,128)(2,1)}) custom-call(bf16[128,7168]{1,0:T(8,128)(2,1)} %tok_ref.1, bf16[128,7168]{1,0:T(8,128)(2,1)} %dy_ref.3, s32[128,8]{1,0:T(8,128)} %copy.15.routes_ref, f32[128,8]{1,0:T(8,128)} %copy.16.weight_ref, ...), custom_call_target="tpu_custom_call" | custom-call | tf_op jit(solution)/shard_map/pallas_call | solution.py:420
  92.8 11.9 %shard_map.119 = (bf16[128,7168]{1,0:T(8,128)(2,1)}, bf16[128,7168]{1,0:T(8,128)(2,1)}, f32[128,8]{1,0:T(8,128)}, bf16[1792,1024]{1,0:T(8,128)(2,1)}, bf16[1792,...) custom-call(s32[128,8]{1,0:T(8,128)} %copy.15.routes_ref, f32[128,8]{1,0:T(8,128)} %copy.16.weight_ref, ...), custom_call_target="tpu_custom_call" | custom-call | tf_op jit(solution)/shard_map/pallas_call | solution.py:466
  104.7 1.5 %copy.17 = f32[128,8]{0,1:T(8,128)} copy(f32[128,8]{1,0:T(8,128)} %get-tuple-element.28) | data formatting | bytes 8192

commit v2 on v1

v2 whole, which is shorter than its diff:
```python
import functools

import jax
import jax.numpy as jnp
from jax import lax
from jax.experimental import pallas as pl
from jax.experimental.pallas import tpu as pltpu
from jax.sharding import PartitionSpec as P

CAP = 6
PARTS = 2
SLOTS = CAP // PARTS
PIECES = 2
ROWS = 16
LANES = 128
MESH = pl.DeviceIdType.MESH
F32 = jnp.float32
BF16 = jnp.bfloat16
VMEM_BYTES = 60 * 1024 * 1024


def block_cols(slice_width):
    tiles = slice_width // LANES
    cols = -(-2 * SLOTS * tiles // ROWS)
    rest = tiles - 2 * cols
    assert 0 <= 2 * rest <= cols
    return cols, rest


def dot(a, b):
    return jnp.dot(a, b, preferred_element_type=F32)


def dot_nt(a, b):
    return lax.dot_general(a, b, (((1,), (1,)), ((), ())), preferred_element_type=F32)


def dot_tn(a, b):
    return lax.dot_general(a, b, (((0,), (0,)), ((), ())), preferred_element_type=F32)


def iota(shape, dim):
    return lax.broadcasted_iota(jnp.int32, shape, dim)


def tile_cols(value, start, count):
    return value[:, start * LANES : (start + count) * LANES]


def slot_in_part(i):
    return jnp.where(
        i < 3, i, jnp.where(i < 6, i - 3, jnp.where(i < 9, i - 6, jnp.where(i < 12, i - 9, i - 12)))
    )


def exchange_kernel(
    experts, heads,
    tok_hbm, dy_hbm, routes_ref, weight_ref, gate_hbm, up_hbm, down_hbm,
    xt_hbm, d_hbm, act_hbm, hidt_hbm, weighted_hbm, plain_hbm, back_hbm,
    tok_ref, dy_ref, gate_w, up_w, down_w, gate_t, up_t, down_t,
    x_ref, d_ref, act_ref, xt_ref, hidt_ref, weighted, plain,
    send1, recv1, send2, pair_send, pair_recv, y_send, y_recv,
    t_sem, w_sem, o_sem, own_sem, s1_sem, r1_sem, s2_sem, r2_sem,
    ps_sem, pr_sem, ys_sem, yr_sem, as_sem, ar_sem,
):
    total = experts * heads
    cores, y_size = 2, heads // 2
    ctx, head = lax.axis_index("ctx"), lax.axis_index("head")
    me = ctx * heads + head
    core, y = head % cores, head // cores
    toks = tok_ref.shape[0]
    picks = routes_ref.shape[0]
    slice_width, hidden = gate_w.shape
    half = hidden // 2
    piece = half // PIECES
    cols, rest = block_cols(slice_width)
    part_rows = total * SLOTS
    group_rows = 16 * SLOTS
    sibling = {"ctx": ctx, "head": y * cores + 1 - core}

    def local(pairs, sem):
        return [pltpu.make_async_copy(src, dst, sem.at[n]) for n, (src, dst) in enumerate(pairs)]

    token_copies = local(((tok_hbm, tok_ref), (dy_hbm, dy_ref)), t_sem)
    weight_copies = local(((gate_hbm, gate_w), (up_hbm, up_w), (down_hbm, down_w)), w_sem)
    for copy in token_copies:
        copy.start()

    barrier = pltpu.get_barrier_semaphore()

    def greet(step, carry):
        j = (me + step) % total
        pl.semaphore_signal(
            barrier, inc=1, device_id={"ctx": j // heads, "head": j % heads}, device_id_type=MESH
        )
        return carry

    lax.fori_loop(1, total, greet, 0)

    routes_t, weight_t = routes_ref[...], weight_ref[...]
    out_rows = experts * ROWS
    row = iota((out_rows, 1), 0)
    row_expert = row // ROWS
    i = row % ROWS
    hit = jnp.zeros((out_rows, toks), F32)
    pick_weight = jnp.zeros((out_rows, toks), F32)
    for k in range(picks):
        same = routes_t[k : k + 1] == row_expert
        hit = jnp.where(same, 1.0, hit)
        pick_weight = jnp.where(same, weight_t[k : k + 1], pick_weight)
    earlier = (iota((toks, toks), 0) < iota((toks, toks), 1)).astype(BF16)
    position = dot(hit.astype(BF16), earlier)

    def choose(part):
        want = (slot_in_part(i) + part * SLOTS).astype(F32)
        return jnp.where((position == want) & (i < 15), hit, 0.0)

    def fill_and_ship(part):
        chosen = choose(part)
        slot_weight = jnp.sum(chosen * pick_weight, axis=1, keepdims=True)
        picked, scale = [], []
        for kind in range(2):
            second = ((i >= 3) & (i < 6)) | ((i >= 9) & (i < 12))
            if kind:
                second = second | (i >= 12)
            picked.append(
                jnp.concatenate(
                    [jnp.where(second, 0.0, chosen), jnp.where(second, chosen, 0.0)], axis=1
                ).astype(BF16)
            )
            scale.append(jnp.where(second, slot_weight, 1.0))
        for turn in range(heads):
            h = (head + turn) % heads
            width = pl.ds(pl.multiple_of(h * slice_width, LANES), slice_width)
            source = jnp.concatenate([tok_ref[:, width], dy_ref[:, width]], axis=0)
            full = dot(picked[0], source) * scale[0]
            tail = dot(picked[1], tile_cols(source, 2 * cols, rest)) * scale[1]
            for j in range(cols):
                value = jnp.where(i < 6, tile_cols(full, j, 1), tile_cols(full, cols + j, 1))
                if j < 2 * rest:
                    last = tile_cols(tail, j // 2, 1) if j % 2 else tile_cols(full, 2 * cols + j // 2, 1)
                    value = jnp.where(i < 12, value, last)
                send1[part, h, :, :, j * LANES : (j + 1) * LANES] = value.astype(BF16).reshape(
                    experts, ROWS, LANES
                )
            if part == 0 and turn == 0:
                pl.semaphore_wait(barrier, total - 1)

            def one(step, carry):
                e = (ctx + step) % experts
                pltpu.make_async_remote_copy(
                    src_ref=send1.at[part, h, e],
                    dst_ref=recv1.at[part, me],
                    send_sem=s1_sem.at[part],
                    recv_sem=r1_sem.at[part],
                    device_id={"ctx": e, "head": h},
                    device_id_type=MESH,
                ).start()
                return carry

            if turn == 0:
                pltpu.make_async_copy(
                    send1.at[part, head, ctx], recv1.at[part, me], own_sem.at[part]
                ).start()
            lax.fori_loop(0 if turn else 1, experts, one, 0)

    def wait_blocks(part, sem):
        blocks = recv1.at[part, pl.ds(0, total - 1)]
        pltpu.make_async_copy(blocks, blocks, sem.at[part]).wait()

    for copy in token_copies:
        copy.wait()
    for copy in weight_copies:
        copy.start()
    for part in range(PARTS):
        fill_and_ship(part)
    for copy in weight_copies:
        copy.wait()

    def flip(n, carry):
        at = pl.ds(pl.multiple_of(n * LANES, LANES), LANES)
        gate_t[:, at] = gate_w[at, :].T
        up_t[:, at] = up_w[at, :].T
        down_t[at, :] = down_w[:, at].T
        return carry

    lax.fori_loop(0, slice_width // LANES, flip, 0)

    for part in range(PARTS):
        chosen = choose(part)
        scaled = chosen * pick_weight
        high = scaled.astype(BF16).astype(F32)
        low = scaled - high
        for band in range(3):
            first = (i >= 6 * band) & (i < 6 * band + 3)
            second = first if band == 2 else (i >= 6 * band + 3) & (i < 6 * band + 6)
            weighted[part, band, :, :out_rows] = jnp.where(first, high, 0.0).T.astype(BF16)
            weighted[part, band, :, out_rows:] = jnp.where(first, low, 0.0).T.astype(BF16)
            plain[band, :, part * out_rows : (part + 1) * out_rows] = jnp.where(
                second, chosen, 0.0
            ).T.astype(BF16)

    def places(first, rows_out):
        out, col = iota((rows_out, 16 * ROWS), 0), iota((rows_out, 16 * ROWS), 1)
        kind = (out >= group_rows).astype(jnp.int32)
        slot = out - kind * group_rows
        return (col == (slot // 3) * ROWS + slot % 3 + kind * 3 + first).astype(BF16)

    place = [places(0, 2 * group_rows), places(6, 2 * group_rows), places(12, group_rows)]

    def activate(part, p, sums):
        gate, up, back = (sums[:, n * piece : (n + 1) * piece] for n in range(3))
        sig = jax.nn.sigmoid(gate)
        smooth = gate * sig
        slope = sig * (1.0 + gate * (1.0 - sig))
        act_ref[part, core, p, :, :piece] = (smooth * up).astype(BF16)
        act_ref[part, core, p, :, piece : 2 * piece] = (back * up * slope).astype(BF16)
        act_ref[part, core, p, :, 2 * piece :] = (back * smooth).astype(BF16)

    def units_of(side, p):
        return pl.ds(pl.multiple_of(side * half + p * piece, piece), piece)

    def project(x, d, side, p):
        units = units_of(side, p)
        return dot(x, gate_w[:, units]), dot(x, up_w[:, units]), dot(d, down_t[:, units])

    def work(part, carry):
        pltpu.make_async_copy(
            send1.at[part, head, ctx], recv1.at[part, me], own_sem.at[part]
        ).wait()
        wait_blocks(part, r1_sem)
        for g in range(total // 16):
            block = recv1[part, pl.ds(g * 16, 16)].reshape(16 * ROWS, cols * LANES)
            at = pl.ds(pl.multiple_of(part * part_rows + g * group_rows, 16), group_rows)
            for band in range(2):
                value = dot(place[band], block).astype(BF16)
                span = pl.ds(band * cols * LANES, cols * LANES)
                x_ref[at, span] = value[:group_rows]
                d_ref[at, span] = value[group_rows:]
            tail = dot(place[2], tile_cols(block, 0, 2 * rest)).astype(BF16)
            for q in range(rest):
                span = pl.ds((2 * cols + q) * LANES, LANES)
                x_ref[at, span] = tile_cols(tail, 2 * q, 1)
                d_ref[at, span] = tile_cols(tail, 2 * q + 1, 1)

        at = pl.ds(pl.multiple_of(part * part_rows, 16), part_rows)
        x, d = x_ref[at, :], d_ref[at, :]
        to_pair, to_y, to_act = [], [], []
        for p in range(PIECES):
            for n, value in enumerate(project(x, d, 1 - core, p)):
                pair_send[part, p, :, n * piece : (n + 1) * piece] = value
            to_pair.append(
                pltpu.make_async_remote_copy(
                    src_ref=pair_send.at[part, p],
                    dst_ref=pair_recv.at[part, p],
                    send_sem=ps_sem.at[part, p],
                    recv_sem=pr_sem.at[part, p],
                    device_id=sibling,
                    device_id_type=MESH,
                )
            )
            to_pair[-1].start()
        sums = []
        for p in range(PIECES):
            mine = jnp.concatenate(project(x, d, core, p), axis=1)
            to_pair[p].wait_recv()
            mine = mine + pair_recv[part, p]
            sums.append(mine)
            y_send[part, p] = mine.astype(BF16)
            to_y.append([])
            for q in range(1, y_size):
                to_y[-1].append(
                    pltpu.make_async_remote_copy(
                        src_ref=y_send.at[part, p],
                        dst_ref=y_recv.at[part, p, q - 1],
                        send_sem=ys_sem.at[part, p, q - 1],
                        recv_sem=yr_sem.at[part, p, q - 1],
                        device_id={"ctx": ctx, "head": ((y + q) % y_size) * cores + core},
                        device_id_type=MESH,
                    )
                )
                to_y[-1][-1].start()
        for p in range(PIECES):
            mine = sums[p]
            for q, copy in enumerate(to_y[p]):
                copy.wait_recv()
                mine = mine + y_recv[part, p, q].astype(F32)
            activate(part, p, mine)
            to_act.append(
                pltpu.make_async_remote_copy(
                    src_ref=act_ref.at[part, core, p],
                    dst_ref=act_ref.at[part, core, p],
                    send_sem=as_sem.at[part, p],
                    recv_sem=ar_sem.at[part, p],
                    device_id=sibling,
                    device_id_type=MESH,
                )
            )
            to_act[-1].start()

        out, grad = 0.0, 0.0
        for far in range(2):
            side = 1 - core if far else core
            for p in range(PIECES):
                if far:
                    to_act[p].wait_recv()
                units = units_of(side, p)
                out += dot(act_ref[part, side, p, :, :piece], down_w[units, :])
                grad += dot(act_ref[part, side, p, :, piece : 2 * piece], gate_t[units, :])
                grad += dot(act_ref[part, side, p, :, 2 * piece :], up_t[units, :])
        out, grad = out.astype(BF16), grad.astype(BF16)
        for g in range(total // 16):
            rows = slice(g * group_rows, (g + 1) * group_rows)
            both = jnp.concatenate([out[rows], grad[rows]], axis=0)
            block = dot_tn(place[0], tile_cols(both, 0, cols)) + dot_tn(
                place[1], tile_cols(both, cols, cols)
            )
            tail = []
            for q in range(rest):
                tail += [tile_cols(v, 2 * cols + q, 1) for v in (out[rows], grad[rows])]
            tail = dot_tn(place[2], jnp.concatenate(tail, axis=1))
            span = 2 * rest * LANES
            block = block.reshape(16, ROWS, cols * LANES)
            send2[part, pl.ds(g * 16, 16), :, :span] = (
                block[:, :, :span] + tail.reshape(16, ROWS, span)
            ).astype(BF16)
            if span < cols * LANES:
                send2[part, pl.ds(g * 16, 16), :, span:] = block[:, :, span:].astype(BF16)

        pltpu.make_async_copy(
            send2.at[part, me], back_hbm.at[part, me], own_sem.at[PARTS + part]
        ).start()

        def one(step, inner):
            j = (me + step) % total
            pltpu.make_async_remote_copy(
                src_ref=send2.at[part, j],
                dst_ref=back_hbm.at[part, me],
                send_sem=s2_sem.at[part],
                recv_sem=r2_sem.at[part],
                device_id={"ctx": j // heads, "head": j % heads},
                device_id_type=MESH,
            ).start()
            return inner

        lax.fori_loop(1, total, one, 0)
        for p in range(PIECES):
            to_pair[p].wait_send()
            for copy in to_y[p]:
                copy.wait_send()
            to_act[p].wait_send()
        return carry

    lax.fori_loop(0, PARTS, work, 0)

    xt_ref[...] = x_ref[...].T
    for side in range(2):
        for p in range(PIECES):
            start = side * half + p * piece
            hidt_ref[start : start + piece, :] = jnp.concatenate(
                [act_ref[part, side, p, :, :piece] for part in range(PARTS)], axis=0
            ).T
    out_copies = local(
        (
            (xt_ref, xt_hbm), (d_ref, d_hbm), (act_ref, act_hbm), (hidt_ref, hidt_hbm),
            (weighted, weighted_hbm), (plain, plain_hbm),
        ),
        o_sem,
    )
    for copy in out_copies:
        copy.start()
    for part in range(PARTS):
        wait_blocks(part, s1_sem)
        wait_blocks(part, s2_sem)
        pltpu.make_async_copy(
            send2.at[part, me], back_hbm.at[part, me], own_sem.at[PARTS + part]
        ).wait()
    for copy in out_copies:
        copy.wait()
    for part in range(PARTS):
        wait_blocks(part, r2_sem)


def finish_kernel(
    experts,
    routes_ref, dy_ref, back_ref, xt_ref, d_ref, act_ref, hidt_ref, weighted, plain,
    moe_ref, grad_tok_ref, grad_route_ref, gate_ref, up_ref, down_ref,
    inner,
):
    step = pl.program_id(0)
    picks = routes_ref.shape[0]
    slice_width = dy_ref.shape[1]
    cols, rest = block_cols(slice_width)
    width = experts * ROWS

    @pl.when(step == 0)
    def _():
        inner[...] = jnp.zeros_like(inner)

    count = down_ref.shape[0]
    piece = act_ref.shape[4] // 3
    piece_steps = piece // count
    slab, offset = step // piece_steps, (step % piece_steps) * count

    def units(start):
        at = pl.ds(pl.multiple_of(start * piece + offset, count), count)
        return jnp.concatenate(
            [act_ref[part, slab // PIECES, slab % PIECES, :, at] for part in range(PARTS)], axis=0
        )

    gate_ref[...] = dot(xt_ref[...], units(1)).astype(BF16)
    up_ref[...] = dot(xt_ref[...], units(2)).astype(BF16)
    down_ref[...] = dot(hidt_ref[...], d_ref[...]).astype(BF16)

    blocks = [back_ref[part, :, 0].reshape(width, cols * LANES) for part in range(PARTS)]
    odd = [jnp.concatenate([tile_cols(b, 2 * q + 1, 1) for q in range(rest)], axis=1) for b in blocks]
    even = [jnp.concatenate([tile_cols(b, 2 * q, 1) for q in range(rest)], axis=1) for b in blocks]
    for band, firsts, seconds, start, count in (
        (0, blocks, blocks, 0, cols),
        (1, blocks, blocks, cols, cols),
        (2, even, odd, 2 * cols, rest),
    ):
        span = slice(start * LANES, (start + count) * LANES)
        moe = 0.0
        for part in range(PARTS):
            moe += dot(weighted[part, band], jnp.concatenate([firsts[part]] * 2, axis=0))
            inner[part, band] += dot_nt(dy_ref[:, span], firsts[part])
        moe_ref[:, span] = moe.astype(BF16)
        grad_tok_ref[:, span] = dot(plain[band], jnp.concatenate(seconds, axis=0)).astype(BF16)

    @pl.when(step == pl.num_programs(0) - 1)
    def _():
        found = 0.0
        for part in range(PARTS):
            for band in range(3):
                chosen = weighted[part, band, :, :width].astype(F32) > 0.0
                found += jnp.where(chosen, inner[part, band], 0.0)
        found = found.T
        row_expert = iota((width, 1), 0) // ROWS
        for k in range(picks):
            grad_route_ref[k : k + 1, :] = jnp.sum(
                jnp.where(routes_ref[k : k + 1, :] == row_expert, found, 0.0), axis=0, keepdims=True
            )


def on_device(tokens, routes, route_weight, w_gate, w_up, w_down, grad_out):
    experts = lax.axis_size("ctx")
    heads = lax.axis_size("head")
    total = experts * heads
    toks, model_width = tokens.shape
    picks = routes.shape[1]
    slice_width, hidden = w_gate.shape[1:]
    half = hidden // 2
    cols, rest = block_cols(slice_width)
    part_rows = total * SLOTS
    all_rows = PARTS * part_rows
    y_others = max(1, heads // 2 - 1)
    piece = half // PIECES
    slots = experts * ROWS
    vmem = pl.BlockSpec(memory_space=pltpu.VMEM)
    hbm = pl.BlockSpec(memory_space=pl.ANY)
    block = (ROWS, cols * LANES)
    dma = pltpu.SemaphoreType.DMA
    handed = (
        (slice_width, all_rows),
        (all_rows, slice_width),
        (PARTS, 2, PIECES, part_rows, 3 * piece),
        (hidden, all_rows),
        (PARTS, 3, toks, 2 * slots),
        (3, toks, PARTS * slots),
    )
    xt, d_rows, acts, hidt, weighted, plain, back = pl.pallas_call(
        functools.partial(exchange_kernel, experts, heads),
        out_shape=tuple(
            jax.ShapeDtypeStruct(shape, BF16) for shape in handed + ((PARTS, total) + block,)
        ),
        in_specs=[hbm] * 2 + [vmem] * 2 + [hbm] * 3,
        out_specs=(hbm,) * 7,
        scratch_shapes=[
            pltpu.VMEM((toks, model_width), BF16),
            pltpu.VMEM((toks, model_width), BF16),
            pltpu.VMEM((slice_width, hidden), BF16),
            pltpu.VMEM((slice_width, hidden), BF16),
            pltpu.VMEM((hidden, slice_width), BF16),
            pltpu.VMEM((hidden, slice_width), BF16),
            pltpu.VMEM((hidden, slice_width), BF16),
            pltpu.VMEM((slice_width, hidden), BF16),
            pltpu.VMEM(handed[1], BF16),
            pltpu.VMEM(handed[1], BF16),
            pltpu.VMEM(handed[2], BF16),
            pltpu.VMEM(handed[0], BF16),
            pltpu.VMEM(handed[3], BF16),
            pltpu.VMEM(handed[4], BF16),
            pltpu.VMEM(handed[5], BF16),
            pltpu.VMEM((PARTS, heads, experts) + block, BF16),
            pltpu.VMEM((PARTS, total) + block, BF16),
            pltpu.VMEM((PARTS, total) + block, BF16),
            pltpu.VMEM((PARTS, PIECES, part_rows, 3 * piece), F32),
            pltpu.VMEM((PARTS, PIECES, part_rows, 3 * piece), F32),
            pltpu.VMEM((PARTS, PIECES, part_rows, 3 * piece), BF16),
            pltpu.VMEM((PARTS, PIECES, y_others, part_rows, 3 * piece), BF16),
            dma((2,)),
            dma((3,)),
            dma((6,)),
            dma((2 * PARTS,)),
            dma((PARTS,)),
            dma((PARTS,)),
            dma((PARTS,)),
            dma((PARTS,)),
            dma((PARTS, PIECES)),
            dma((PARTS, PIECES)),
            dma((PARTS, PIECES, y_others)),
            dma((PARTS, PIECES, y_others)),
            dma((PARTS, PIECES)),
            dma((PARTS, PIECES)),
        ],
        compiler_params=pltpu.CompilerParams(
            collective_id=0, has_side_effects=True, vmem_limit_bytes=VMEM_BYTES
        ),
    )(tokens, grad_out, routes.T, route_weight.T, w_gate[0], w_up[0], w_down[0])

    back = back.reshape((PARTS, experts, heads) + block)

    def whole(shape):
        return pl.BlockSpec(shape, lambda h: (0,) * len(shape))

    units = hidden // heads
    moe_out, grad_tokens, grad_route, grad_gate, grad_up, grad_down = pl.pallas_call(
        functools.partial(finish_kernel, experts),
        grid=(heads,),
        in_specs=[
            whole((picks, toks)),
            pl.BlockSpec((toks, slice_width), lambda h: (0, h)),
            pl.BlockSpec((PARTS, experts, 1) + block, lambda h: (0, 0, h, 0, 0)),
            whole(handed[0]),
            whole(handed[1]),
            whole(handed[2]),
            pl.BlockSpec((units, all_rows), lambda h: (h, 0)),
            whole(handed[4]),
            whole(handed[5]),
        ],
        out_specs=(
            pl.BlockSpec((toks, slice_width), lambda h: (0, h)),
            pl.BlockSpec((toks, slice_width), lambda h: (0, h)),
            whole((picks, toks)),
            pl.BlockSpec((slice_width, units), lambda h: (0, h)),
            pl.BlockSpec((slice_width, units), lambda h: (0, h)),
            pl.BlockSpec((units, slice_width), lambda h: (h, 0)),
        ),
        out_shape=(
            jax.ShapeDtypeStruct((toks, model_width), BF16),
            jax.ShapeDtypeStruct((toks, model_width), BF16),
            jax.ShapeDtypeStruct((picks, toks), F32),
            jax.ShapeDtypeStruct((slice_width, hidden), BF16),
            jax.ShapeDtypeStruct((slice_width, hidden), BF16),
            jax.ShapeDtypeStruct((hidden, slice_width), BF16),
        ),
        scratch_shapes=[pltpu.VMEM((PARTS, 3, toks, slots), F32)],
        compiler_params=pltpu.CompilerParams(vmem_limit_bytes=VMEM_BYTES),
    )(routes.T, grad_out, back, xt, d_rows, acts, hidt, weighted, plain)
    return (moe_out, grad_tokens, grad_route.T, grad_gate[None], grad_up[None], grad_down[None])


def solution(mesh):
    tok = P(("ctx", "head"), None)
    col, row = P("ctx", "head", None), P("ctx", None, "head")
    return jax.shard_map(
        on_device,
        mesh=mesh,
        in_specs=(tok, tok, tok, col, col, row, tok),
        out_specs=(tok, tok, tok, col, col, row),
        check_vma=False,
    )
```

time: 106 us -> 97.5 us (0.920)
  Pallas kernels: 101 us -> 96.6 us
  local copies, waits for them, and re-layouts: 4.32 us -> 0 us
    unnamed x3 -> x0, local copies, waits for them, and re-layouts: 4.32 us -> none
    pallas_call x1, Pallas kernels: 89.3 us -> 85.7 us  [on_device(): pl.pallas_call(functools.partial(exchange_kernel, experts, heads), out_sh...]
where the time goes in v2:
time: 97.5 us; the launch traced here: 97.3 us
  Pallas kernels  96.6 us (99%)
    pallas_call x1, Pallas kernels, on_device(): pl.pallas_call(functools.partial(exchange_kernel, experts, heads), out_sh...  85.7 us
    pallas_call x1, Pallas kernels, on_device(): pl.pallas_call(functools.partial(finish_kernel, experts), grid=(heads,),...  10.9 us

profile of v2, /device:TPU:27, one launch (start us, length us, event | category | flops | bytes accessed | tf_op | source)
XLA Modules:
  0.0 97.3 jit_solution(8411422941849054250)
XLA Ops:
  0.6 85.7 %shard_map.118 = (bf16[1792,192]{1,0:T(8,128)(2,1)}, bf16[192,1792]{1,0:T(8,128)(2,1)}, bf16[2,2,2,96,768]{4,3,2,1,0:T(8,128)(2,1)}, bf16[1024,192]{1,0:T(8,128)...) custom-call(bf16[128,7168]{1,0:T(8,128)(2,1)} %tok_hbm.1, ...), custom_call_target="tpu_custom_call" | custom-call | tf_op jit(solution)/shard_map/pallas_call | solution.py:472
  86.4 10.9 %shard_map.119 = (bf16[128,7168]{1,0:T(8,128)(2,1)}, bf16[128,7168]{1,0:T(8,128)(2,1)}, f32[8,128]{1,0:T(8,128)}, bf16[1792,1024]{1,0:T(8,128)(2,1)}, bf16[1792,...) custom-call(s32[8,128]{1,0:T(8,128)} %bitcast.15, bf16[128,7168]{1,0:T(8,128)(2,1)} %dy_ref.1, ...), custom_call_target="tpu_custom_call" | custom-call | tf_op jit(solution)/shard_map/pallas_call | solution.py:528

commit v3 on v2

v3 whole, which is shorter than its diff:
```python
import functools

import jax
import jax.numpy as jnp
from jax import lax
from jax.experimental import pallas as pl
from jax.experimental.pallas import tpu as pltpu
from jax.sharding import PartitionSpec as P

CAP = 6
SPLIT = (4, 2)
PARTS = len(SPLIT)
PIECES = 2
ROWS = 16
LANES = 128
MESH = pl.DeviceIdType.MESH
F32 = jnp.float32
BF16 = jnp.bfloat16
VMEM_BYTES = 60 * 1024 * 1024


class Form:
    def __init__(self, part, slice_width):
        self.slots = SPLIT[part]
        self.first = sum(SPLIT[:part])
        self.height = 2 * self.slots
        self.bands = ROWS // self.height
        tiles = slice_width // LANES
        self.cols = -(-tiles // self.bands)
        self.block = (ROWS, self.cols * LANES)
        self.spans = [
            (b * self.cols, min(self.cols, tiles - b * self.cols)) for b in range(self.bands)
        ]


def forms(slice_width):
    return [Form(part, slice_width) for part in range(PARTS)]


def dot(a, b):
    return jnp.dot(a, b, preferred_element_type=F32)


def dot_nt(a, b):
    return lax.dot_general(a, b, (((1,), (1,)), ((), ())), preferred_element_type=F32)


def iota(shape, dim):
    return lax.broadcasted_iota(jnp.int32, shape, dim)


def tile_cols(value, start, count):
    return value[:, start * LANES : (start + count) * LANES]


def exchange_kernel(
    experts, heads,
    tok_hbm, dy_hbm, routes_ref, weight_ref, gate_hbm, up_hbm, down_hbm,
    xt_hbm, d_hbm, act_hbm, hidt_hbm, select_hbm, back0_hbm, back1_hbm,
    tok_ref, dy_ref, gate_w, up_w, down_w, gate_t, up_t, down_t,
    x_ref, d_ref, act_ref, xt_ref, hidt_ref, select,
    out0, out1, in0, in1, ret0, ret1, pair_send, pair_recv, y_send, y_recv,
    t_sem, w_sem, o_sem, own_sem, s1_sem, r1_sem, s2_sem, r2_sem,
    ps_sem, pr_sem, ys_sem, yr_sem, as_sem, ar_sem,
):
    total = experts * heads
    cores, y_size = 2, heads // 2
    ctx, head = lax.axis_index("ctx"), lax.axis_index("head")
    me = ctx * heads + head
    core, y = head % cores, head // cores
    toks = tok_ref.shape[0]
    picks = routes_ref.shape[0]
    slice_width, hidden = gate_w.shape
    half = hidden // 2
    piece = half // PIECES
    form = forms(slice_width)
    send1, recv1, send2, back = (out0, out1), (in0, in1), (ret0, ret1), (back0_hbm, back1_hbm)
    sibling = {"ctx": ctx, "head": y * cores + 1 - core}

    def local(pairs, sem):
        return [pltpu.make_async_copy(src, dst, sem.at[n]) for n, (src, dst) in enumerate(pairs)]

    token_copies = local(((tok_hbm, tok_ref), (dy_hbm, dy_ref)), t_sem)
    weight_copies = local(((gate_hbm, gate_w), (up_hbm, up_w), (down_hbm, down_w)), w_sem)
    for copy in token_copies:
        copy.start()

    barrier = pltpu.get_barrier_semaphore()

    def greet(step, carry):
        j = (me + step) % total
        pl.semaphore_signal(
            barrier, inc=1, device_id={"ctx": j // heads, "head": j % heads}, device_id_type=MESH
        )
        return carry

    lax.fori_loop(1, total, greet, 0)

    routes_t, weight_t = routes_ref[...], weight_ref[...]
    out_rows = experts * ROWS
    row = iota((out_rows, 1), 0)
    row_expert = row // ROWS
    i = row % ROWS
    hit = jnp.zeros((out_rows, toks), F32)
    pick_weight = jnp.zeros((out_rows, toks), F32)
    for k in range(picks):
        same = routes_t[k : k + 1] == row_expert
        hit = jnp.where(same, 1.0, hit)
        pick_weight = jnp.where(same, weight_t[k : k + 1], pick_weight)
    earlier = (iota((toks, toks), 0) < iota((toks, toks), 1)).astype(BF16)
    position = dot(hit.astype(BF16), earlier)

    def choose(f):
        want = (i % f.slots + f.first).astype(F32)
        return jnp.where(position == want, hit, 0.0), i % f.height >= f.slots

    def own_in(part):
        return pltpu.make_async_copy(
            send1[part].at[head, ctx], recv1[part].at[me], own_sem.at[part]
        )

    def own_back(part):
        return pltpu.make_async_copy(
            send2[part].at[ctx, head], back[part].at[me], own_sem.at[PARTS + part]
        )

    def send_turn(part, turn, returning):
        h = (head + turn) % heads

        def one(step, carry):
            e = (ctx + step) % experts
            pltpu.make_async_remote_copy(
                src_ref=send2[part].at[e, h] if returning else send1[part].at[h, e],
                dst_ref=back[part].at[me] if returning else recv1[part].at[me],
                send_sem=(s2_sem if returning else s1_sem).at[part],
                recv_sem=(r2_sem if returning else r1_sem).at[part],
                device_id={"ctx": e, "head": h},
                device_id_type=MESH,
            ).start()
            return carry

        if turn == 0:
            (own_back if returning else own_in)(part).start()
        lax.fori_loop(0 if turn else 1, experts, one, 0)

    def send_quarters(part, quarters, returning):
        for q in quarters:
            for turn in range(q * heads // 4, (q + 1) * heads // 4):
                send_turn(part, turn, returning)

    def fill(part, picked, scale, turn):
        f = form[part]
        h = (head + turn) % heads
        width = pl.ds(pl.multiple_of(h * slice_width, LANES), slice_width)
        source = jnp.concatenate([tok_ref[:, width], dy_ref[:, width]], axis=0)
        full = dot(picked, source) * scale
        for j in range(f.cols):
            value = tile_cols(full, j, 1)
            for b in range(1, f.bands):
                if j < f.spans[b][1]:
                    value = jnp.where(
                        i < b * f.height, value, tile_cols(full, b * f.cols + j, 1)
                    )
            send1[part][h, :, :, j * LANES : (j + 1) * LANES] = value.astype(BF16).reshape(
                experts, ROWS, LANES
            )

    def wait_blocks(part, sem):
        blocks = recv1[part].at[pl.ds(0, total - 1)]
        pltpu.make_async_copy(blocks, blocks, sem.at[part]).wait()

    for copy in token_copies:
        copy.wait()
    for copy in weight_copies:
        copy.start()
    for part in range(PARTS):
        chosen, second = choose(form[part])
        slot_weight = jnp.sum(chosen * pick_weight, axis=1, keepdims=True)
        picked = jnp.concatenate(
            [jnp.where(second, 0.0, chosen), jnp.where(second, chosen, 0.0)], axis=1
        ).astype(BF16)
        scale = jnp.where(second, slot_weight, 1.0)
        for turn in range(heads):
            fill(part, picked, scale, turn)
            if part == 0:
                if turn == 0:
                    pl.semaphore_wait(barrier, total - 1)
                send_turn(part, turn, False)
    send_quarters(1, (0, 1), False)
    for copy in weight_copies:
        copy.wait()

    def flip(n, carry):
        at = pl.ds(pl.multiple_of(n * LANES, LANES), LANES)
        gate_t[:, at] = gate_w[at, :].T
        up_t[:, at] = up_w[at, :].T
        down_t[at, :] = down_w[:, at].T
        return carry

    lax.fori_loop(0, slice_width // LANES, flip, 0)

    n = 0
    for part in range(PARTS):
        f = form[part]
        chosen, second = choose(f)
        scaled = chosen * pick_weight
        high = scaled.astype(BF16).astype(F32)
        low = scaled - high
        for b in range(f.bands):
            band = i // f.height == b
            first = band & ~second
            select[n, :toks, :out_rows] = jnp.where(first, high, 0.0).T.astype(BF16)
            select[n, :toks, out_rows:] = jnp.where(first, low, 0.0).T.astype(BF16)
            select[n, toks:, :out_rows] = jnp.where(band & second, chosen, 0.0).T.astype(BF16)
            select[n, toks:, out_rows:] = jnp.zeros((toks, out_rows), BF16)
            n += 1

    def place(f, b, turned):
        count = 2 * 16 * f.slots
        shape = (16 * ROWS, count) if turned else (count, 16 * ROWS)
        out, src = iota(shape, int(turned)), iota(shape, 1 - int(turned))
        kind = (out >= count // 2).astype(jnp.int32)
        slot = out - kind * (count // 2)
        from_row = (slot // f.slots) * ROWS + slot % f.slots + kind * f.slots + b * f.height
        return (src == from_row).astype(BF16)

    def activate(rows, p, sums):
        gate, up, back_grad = (sums[:, n * piece : (n + 1) * piece] for n in range(3))
        sig = jax.nn.sigmoid(gate)
        smooth = gate * sig
        slope = sig * (1.0 + gate * (1.0 - sig))
        act_ref[core, p, rows, :piece] = (smooth * up).astype(BF16)
        act_ref[core, p, rows, piece : 2 * piece] = (back_grad * up * slope).astype(BF16)
        act_ref[core, p, rows, 2 * piece :] = (back_grad * smooth).astype(BF16)

    def units_of(side, p):
        return pl.ds(pl.multiple_of(side * half + p * piece, piece), piece)

    def project(x, d, side, p):
        units = units_of(side, p)
        return dot(x, gate_w[:, units]), dot(x, up_w[:, units]), dot(d, down_t[:, units])

    def work(part, beside_sums, beside_acts):
        f = form[part]
        rows = pl.ds(f.first * total, f.slots * total)
        group_rows = 16 * f.slots
        own_in(part).wait()
        wait_blocks(part, r1_sem)
        places = [place(f, b, False) for b in range(f.bands)]
        for g in range(total // 16):
            block = recv1[part][pl.ds(g * 16, 16)].reshape(16 * ROWS, f.cols * LANES)
            at = pl.ds(f.first * total + g * group_rows, group_rows)
            for b, (start, count) in enumerate(f.spans):
                value = dot(places[b], tile_cols(block, 0, count)).astype(BF16)
                span = pl.ds(start * LANES, count * LANES)
                x_ref[at, span] = value[:group_rows]
                d_ref[at, span] = value[group_rows:]

        x, d = x_ref[rows, :], d_ref[rows, :]
        to_pair, to_y, to_act = [], [], []
        for p in range(PIECES):
            for n, value in enumerate(project(x, d, 1 - core, p)):
                pair_send[p, rows, n * piece : (n + 1) * piece] = value
            to_pair.append(
                pltpu.make_async_remote_copy(
                    src_ref=pair_send.at[p, rows],
                    dst_ref=pair_recv.at[p, rows],
                    send_sem=ps_sem.at[part, p],
                    recv_sem=pr_sem.at[part, p],
                    device_id=sibling,
                    device_id_type=MESH,
                )
            )
            to_pair[-1].start()
        sums = []
        for p in range(PIECES):
            mine = jnp.concatenate(project(x, d, core, p), axis=1)
            to_pair[p].wait_recv()
            mine = mine + pair_recv[p, rows]
            sums.append(mine)
            y_send[p, rows] = mine.astype(BF16)
            to_y.append([])
            for q in range(1, y_size):
                to_y[-1].append(
                    pltpu.make_async_remote_copy(
                        src_ref=y_send.at[p, rows],
                        dst_ref=y_recv.at[q - 1, p, rows],
                        send_sem=ys_sem.at[part, p, q - 1],
                        recv_sem=yr_sem.at[part, p, q - 1],
                        device_id={"ctx": ctx, "head": ((y + q) % y_size) * cores + core},
                        device_id_type=MESH,
                    )
                )
                to_y[-1][-1].start()
        beside_sums()
        for p in range(PIECES):
            mine = sums[p]
            for q, copy in enumerate(to_y[p]):
                copy.wait_recv()
                mine = mine + y_recv[q, p, rows].astype(F32)
            activate(rows, p, mine)
            to_act.append(
                pltpu.make_async_remote_copy(
                    src_ref=act_ref.at[core, p, rows],
                    dst_ref=act_ref.at[core, p, rows],
                    send_sem=as_sem.at[part, p],
                    recv_sem=ar_sem.at[part, p],
                    device_id=sibling,
                    device_id_type=MESH,
                )
            )
            to_act[-1].start()
        beside_acts()

        out, grad = 0.0, 0.0
        for far in range(2):
            side = 1 - core if far else core
            for p in range(PIECES):
                if far:
                    to_act[p].wait_recv()
                units = units_of(side, p)
                out += dot(act_ref[side, p, rows, :piece], down_w[units, :])
                grad += dot(act_ref[side, p, rows, piece : 2 * piece], gate_t[units, :])
                grad += dot(act_ref[side, p, rows, 2 * piece :], up_t[units, :])
        out, grad = out.astype(BF16), grad.astype(BF16)
        places = [place(f, b, True) for b in range(f.bands)]
        for g in range(total // 16):
            at = slice(g * group_rows, (g + 1) * group_rows)
            both = jnp.concatenate([out[at], grad[at]], axis=0)
            block = 0.0
            for b, (start, count) in enumerate(f.spans):
                band = dot(places[b], tile_cols(both, start, count))
                if count < f.cols:
                    gap = jnp.zeros((16 * ROWS, (f.cols - count) * LANES), F32)
                    band = jnp.concatenate([band, gap], axis=1)
                block += band
            send2[part][pl.ds(g * 16 // heads, 16 // heads)] = block.astype(BF16).reshape(
                (16 // heads, heads) + f.block
            )
        return to_pair + sum(to_y, []) + to_act

    started = work(
        0, lambda: send_quarters(1, (2,), False), lambda: send_quarters(1, (3,), False)
    )
    send_quarters(0, (0,), True)
    started += work(
        1, lambda: send_quarters(0, (1,), True), lambda: send_quarters(0, (2, 3), True)
    )
    send_quarters(1, range(4), True)

    xt_ref[...] = x_ref[...].T
    for side in range(2):
        for p in range(PIECES):
            start = side * half + p * piece
            hidt_ref[start : start + piece, :] = act_ref[side, p, :, :piece].T
    out_copies = local(
        (
            (xt_ref, xt_hbm), (d_ref, d_hbm), (act_ref, act_hbm), (hidt_ref, hidt_hbm),
            (select, select_hbm),
        ),
        o_sem,
    )
    for copy in out_copies:
        copy.start()
    for copy in started:
        copy.wait_send()
    for part in range(PARTS):
        wait_blocks(part, s1_sem)
        wait_blocks(part, s2_sem)
        own_back(part).wait()
    for copy in out_copies:
        copy.wait()
    for part in range(PARTS):
        wait_blocks(part, r2_sem)


def finish_kernel(
    experts,
    routes_ref, dy_ref, back0_ref, back1_ref, xt_ref, d_ref, act_ref, hidt_ref, select,
    moe_ref, grad_tok_ref, grad_route_ref, gate_ref, up_ref, down_ref,
    inner,
):
    step = pl.program_id(0)
    picks, toks = routes_ref.shape
    slice_width = dy_ref.shape[1]
    width = experts * ROWS

    @pl.when(step == 0)
    def _():
        inner[...] = jnp.zeros_like(inner)

    count = down_ref.shape[0]
    piece = act_ref.shape[3] // 3
    piece_steps = piece // count
    slab, offset = step // piece_steps, (step % piece_steps) * count

    def units(start):
        at = pl.ds(pl.multiple_of(start * piece + offset, count), count)
        return act_ref[slab // PIECES, slab % PIECES, :, at]

    gate_ref[...] = dot(xt_ref[...], units(1)).astype(BF16)
    up_ref[...] = dot(xt_ref[...], units(2)).astype(BF16)
    down_ref[...] = dot(hidt_ref[...], d_ref[...]).astype(BF16)

    combined, n = 0.0, 0
    for f, back_ref in zip(forms(slice_width), (back0_ref, back1_ref)):
        block = back_ref[:, 0].reshape(width, f.cols * LANES)
        twice = jnp.concatenate([block, block], axis=0)
        bands = []
        for start, count in f.spans:
            bands.append(dot(select[n], tile_cols(twice, 0, count)))
            span = slice(start * LANES, (start + count) * LANES)
            inner[n] += dot_nt(dy_ref[:, span], tile_cols(block, 0, count))
            n += 1
        combined += jnp.concatenate(bands, axis=1)
    moe_ref[...] = combined[:toks].astype(BF16)
    grad_tok_ref[...] = combined[toks:].astype(BF16)

    @pl.when(step == pl.num_programs(0) - 1)
    def _():
        found = 0.0
        for n in range(inner.shape[0]):
            chosen = select[n, :toks, :width].astype(F32) > 0.0
            found += jnp.where(chosen, inner[n], 0.0)
        found = found.T
        row_expert = iota((width, 1), 0) // ROWS
        for k in range(picks):
            grad_route_ref[k : k + 1, :] = jnp.sum(
                jnp.where(routes_ref[k : k + 1, :] == row_expert, found, 0.0), axis=0, keepdims=True
            )


def on_device(tokens, routes, route_weight, w_gate, w_up, w_down, grad_out):
    experts = lax.axis_size("ctx")
    heads = lax.axis_size("head")
    total = experts * heads
    toks, model_width = tokens.shape
    picks = routes.shape[1]
    slice_width, hidden = w_gate.shape[1:]
    all_rows = CAP * total
    y_others = max(1, heads // 2 - 1)
    piece = hidden // 2 // PIECES
    slots = experts * ROWS
    form = forms(slice_width)
    bands = sum(f.bands for f in form)
    vmem = pl.BlockSpec(memory_space=pltpu.VMEM)
    hbm = pl.BlockSpec(memory_space=pl.ANY)
    dma = pltpu.SemaphoreType.DMA
    handed = (
        (slice_width, all_rows),
        (all_rows, slice_width),
        (2, PIECES, all_rows, 3 * piece),
        (hidden, all_rows),
        (bands, 2 * toks, 2 * slots),
    )
    sums = (PIECES, all_rows, 3 * piece)
    xt, d_rows, acts, hidt, select, *back = pl.pallas_call(
        functools.partial(exchange_kernel, experts, heads),
        out_shape=tuple(
            jax.ShapeDtypeStruct(shape, BF16)
            for shape in handed + tuple((total,) + f.block for f in form)
        ),
        in_specs=[hbm] * 2 + [vmem] * 2 + [hbm] * 3,
        out_specs=(hbm,) * 7,
        scratch_shapes=[
            pltpu.VMEM((toks, model_width), BF16),
            pltpu.VMEM((toks, model_width), BF16),
            pltpu.VMEM((slice_width, hidden), BF16),
            pltpu.VMEM((slice_width, hidden), BF16),
            pltpu.VMEM((hidden, slice_width), BF16),
            pltpu.VMEM((hidden, slice_width), BF16),
            pltpu.VMEM((hidden, slice_width), BF16),
            pltpu.VMEM((slice_width, hidden), BF16),
            pltpu.VMEM(handed[1], BF16),
            pltpu.VMEM(handed[1], BF16),
            pltpu.VMEM(handed[2], BF16),
            pltpu.VMEM(handed[0], BF16),
            pltpu.VMEM(handed[3], BF16),
            pltpu.VMEM(handed[4], BF16),
            *(pltpu.VMEM((heads, experts) + f.block, BF16) for f in form),
            *(pltpu.VMEM((total,) + f.block, BF16) for f in form),
            *(pltpu.VMEM((experts, heads) + f.block, BF16) for f in form),
            pltpu.VMEM(sums, F32),
            pltpu.VMEM(sums, F32),
            pltpu.VMEM(sums, BF16),
            pltpu.VMEM((y_others,) + sums, BF16),
            dma((2,)),
            dma((3,)),
            dma((5,)),
            dma((2 * PARTS,)),
            dma((PARTS,)),
            dma((PARTS,)),
            dma((PARTS,)),
            dma((PARTS,)),
            dma((PARTS, PIECES)),
            dma((PARTS, PIECES)),
            dma((PARTS, PIECES, y_others)),
            dma((PARTS, PIECES, y_others)),
            dma((PARTS, PIECES)),
            dma((PARTS, PIECES)),
        ],
        compiler_params=pltpu.CompilerParams(
            collective_id=0, has_side_effects=True, vmem_limit_bytes=VMEM_BYTES
        ),
    )(tokens, grad_out, routes.T, route_weight.T, w_gate[0], w_up[0], w_down[0])

    back = [b.reshape((experts, heads) + f.block) for b, f in zip(back, form)]

    def whole(shape):
        return pl.BlockSpec(shape, lambda h: (0,) * len(shape))

    units = hidden // heads
    moe_out, grad_tokens, grad_route, grad_gate, grad_up, grad_down = pl.pallas_call(
        functools.partial(finish_kernel, experts),
        grid=(heads,),
        in_specs=[
            whole((picks, toks)),
            pl.BlockSpec((toks, slice_width), lambda h: (0, h)),
            *(pl.BlockSpec((experts, 1) + f.block, lambda h: (0, h, 0, 0)) for f in form),
            whole(handed[0]),
            whole(handed[1]),
            whole(handed[2]),
            pl.BlockSpec((units, all_rows), lambda h: (h, 0)),
            whole(handed[4]),
        ],
        out_specs=(
            pl.BlockSpec((toks, slice_width), lambda h: (0, h)),
            pl.BlockSpec((toks, slice_width), lambda h: (0, h)),
            whole((picks, toks)),
            pl.BlockSpec((slice_width, units), lambda h: (0, h)),
            pl.BlockSpec((slice_width, units), lambda h: (0, h)),
            pl.BlockSpec((units, slice_width), lambda h: (h, 0)),
        ),
        out_shape=(
            jax.ShapeDtypeStruct((toks, model_width), BF16),
            jax.ShapeDtypeStruct((toks, model_width), BF16),
            jax.ShapeDtypeStruct((picks, toks), F32),
            jax.ShapeDtypeStruct((slice_width, hidden), BF16),
            jax.ShapeDtypeStruct((slice_width, hidden), BF16),
            jax.ShapeDtypeStruct((hidden, slice_width), BF16),
        ),
        scratch_shapes=[pltpu.VMEM((bands, toks, slots), F32)],
        compiler_params=pltpu.CompilerParams(vmem_limit_bytes=VMEM_BYTES),
    )(routes.T, grad_out, *back, xt, d_rows, acts, hidt, select)
    return (moe_out, grad_tokens, grad_route.T, grad_gate[None], grad_up[None], grad_down[None])


def solution(mesh):
    tok = P(("ctx", "head"), None)
    col, row = P("ctx", "head", None), P("ctx", None, "head")
    return jax.shard_map(
        on_device,
        mesh=mesh,
        in_specs=(tok, tok, tok, col, col, row, tok),
        out_specs=(tok, tok, tok, col, col, row),
        check_vma=False,
    )
```

time: 97.5 us -> 98.4 us (level)
  the two profiles are of different devices: /device:TPU:27 before, /device:TPU:0 now
where the time goes in v3:
time: 98.4 us; the launch traced here: 97.9 us
  Pallas kernels  97.2 us (99%)
    pallas_call x1, Pallas kernels, on_device(): pl.pallas_call(functools.partial(exchange_kernel, experts, heads), out_sh...  85.8 us
    pallas_call x1, Pallas kernels, on_device(): pl.pallas_call(functools.partial(finish_kernel, experts), grid=(heads,),...  11.5 us

profile of v3, /device:TPU:0, one launch (start us, length us, event | category | flops | bytes accessed | tf_op | source)
XLA Modules:
  0.0 97.9 jit_solution(4279188123546529897)
XLA Ops:
  0.6 85.8 %shard_map.118 = (bf16[1792,192]{1,0:T(8,128)(2,1)}, bf16[192,1792]{1,0:T(8,128)(2,1)}, bf16[2,2,192,768]{3,2,1,0:T(8,128)(2,1)}, bf16[1024,192]{1,0:T(8,128)(2,...) custom-call(bf16[128,7168]{1,0:T(8,128)(2,1)} %tok_hbm.1, ...), custom_call_target="tpu_custom_call" | custom-call | tf_op jit(solution)/shard_map/pallas_call | solution.py:457
  86.4 11.5 %shard_map.119 = (bf16[128,7168]{1,0:T(8,128)(2,1)}, bf16[128,7168]{1,0:T(8,128)(2,1)}, f32[8,128]{1,0:T(8,128)}, bf16[1792,1024]{1,0:T(8,128)(2,1)}, bf16[1792,...) custom-call(s32[8,128]{1,0:T(8,128)} %bitcast.17, bf16[128,7168]{1,0:T(8,128)(2,1)} %dy_ref.1, ...), custom_call_target="tpu_custom_call" | custom-call | tf_op jit(solution)/shard_map/pallas_call | solution.py:513

commit v4 on v3

--- a/solution.py
+++ b/solution.py
@@ -10,7 +10,7 @@
 CAP = 6
 SPLIT = (4, 2)
 PARTS = len(SPLIT)
-PIECES = 2
+PIECES = 1
 ROWS = 16
 LANES = 128
 MESH = pl.DeviceIdType.MESH
@@ -57,7 +57,7 @@
     experts, heads,
     tok_hbm, dy_hbm, routes_ref, weight_ref, gate_hbm, up_hbm, down_hbm,
     xt_hbm, d_hbm, act_hbm, hidt_hbm, select_hbm, back0_hbm, back1_hbm,
-    tok_ref, dy_ref, gate_w, up_w, down_w, gate_t, up_t, down_t,
+    tok_ref, dy_ref, pair_w, down_w, pair_t, down_t,
     x_ref, d_ref, act_ref, xt_ref, hidt_ref, select,
     out0, out1, in0, in1, ret0, ret1, pair_send, pair_recv, y_send, y_recv,
     t_sem, w_sem, o_sem, own_sem, s1_sem, r1_sem, s2_sem, r2_sem,
@@ -70,7 +70,7 @@
     core, y = head % cores, head // cores
     toks = tok_ref.shape[0]
     picks = routes_ref.shape[0]
-    slice_width, hidden = gate_w.shape
+    hidden, slice_width = down_w.shape
     half = hidden // 2
     piece = half // PIECES
     form = forms(slice_width)
@@ -81,7 +81,16 @@
         return [pltpu.make_async_copy(src, dst, sem.at[n]) for n, (src, dst) in enumerate(pairs)]
 
     token_copies = local(((tok_hbm, tok_ref), (dy_hbm, dy_ref)), t_sem)
-    weight_copies = local(((gate_hbm, gate_w), (up_hbm, up_w), (down_hbm, down_w)), w_sem)
+    weight_moves = [(down_hbm, down_w)]
+    for slab in range(2 * PIECES):
+        for n, src in enumerate((gate_hbm, up_hbm)):
+            weight_moves.append(
+                (
+                    src.at[:, pl.ds(slab * piece, piece)],
+                    pair_w.at[slab, :, pl.ds(n * piece, piece)],
+                )
+            )
+    weight_copies = local(weight_moves, w_sem)
     for copy in token_copies:
         copy.start()
 
@@ -143,10 +152,9 @@
             (own_back if returning else own_in)(part).start()
         lax.fori_loop(0 if turn else 1, experts, one, 0)
 
-    def send_quarters(part, quarters, returning):
-        for q in quarters:
-            for turn in range(q * heads // 4, (q + 1) * heads // 4):
-                send_turn(part, turn, returning)
+    def send_all(part, returning):
+        for turn in range(heads):
+            send_turn(part, turn, returning)
 
     def fill(part, picked, scale, turn):
         f = form[part]
@@ -182,18 +190,16 @@
         scale = jnp.where(second, slot_weight, 1.0)
         for turn in range(heads):
             fill(part, picked, scale, turn)
-            if part == 0:
-                if turn == 0:
-                    pl.semaphore_wait(barrier, total - 1)
-                send_turn(part, turn, False)
-    send_quarters(1, (0, 1), False)
+            if part == 0 and turn == 0:
+                pl.semaphore_wait(barrier, total - 1)
+            send_turn(part, turn, False)
     for copy in weight_copies:
         copy.wait()
 
     def flip(n, carry):
         at = pl.ds(pl.multiple_of(n * LANES, LANES), LANES)
-        gate_t[:, at] = gate_w[at, :].T
-        up_t[:, at] = up_w[at, :].T
+        for slab in range(2 * PIECES):
+            pair_t[slab, :, at] = pair_w[slab, at, :].T
         down_t[at, :] = down_w[:, at].T
         return carry
 
@@ -237,10 +243,9 @@
         return pl.ds(pl.multiple_of(side * half + p * piece, piece), piece)
 
     def project(x, d, side, p):
-        units = units_of(side, p)
-        return dot(x, gate_w[:, units]), dot(x, up_w[:, units]), dot(d, down_t[:, units])
-
-    def work(part, beside_sums, beside_acts):
+        return dot(x, pair_w[side * PIECES + p]), dot(d, down_t[:, units_of(side, p)])
+
+    def work(part):
         f = form[part]
         rows = pl.ds(f.first * total, f.slots * total)
         group_rows = 16 * f.slots
@@ -259,8 +264,9 @@
         x, d = x_ref[rows, :], d_ref[rows, :]
         to_pair, to_y, to_act = [], [], []
         for p in range(PIECES):
-            for n, value in enumerate(project(x, d, 1 - core, p)):
-                pair_send[p, rows, n * piece : (n + 1) * piece] = value
+            ahead, behind = project(x, d, 1 - core, p)
+            pair_send[p, rows, : 2 * piece] = ahead
+            pair_send[p, rows, 2 * piece :] = behind
             to_pair.append(
                 pltpu.make_async_remote_copy(
                     src_ref=pair_send.at[p, rows],
@@ -292,7 +298,6 @@
                     )
                 )
                 to_y[-1][-1].start()
-        beside_sums()
         for p in range(PIECES):
             mine = sums[p]
             for q, copy in enumerate(to_y[p]):
@@ -310,7 +315,6 @@
                 )
             )
             to_act[-1].start()
-        beside_acts()
 
         out, grad = 0.0, 0.0
         for far in range(2):
@@ -320,8 +324,7 @@
                     to_act[p].wait_recv()
                 units = units_of(side, p)
                 out += dot(act_ref[side, p, rows, :piece], down_w[units, :])
-                grad += dot(act_ref[side, p, rows, piece : 2 * piece], gate_t[units, :])
-                grad += dot(act_ref[side, p, rows, 2 * piece :], up_t[units, :])
+                grad += dot(act_ref[side, p, rows, piece:], pair_t[side * PIECES + p])
         out, grad = out.astype(BF16), grad.astype(BF16)
         places = [place(f, b, True) for b in range(f.bands)]
         for g in range(total // 16):
@@ -339,14 +342,10 @@
             )
         return to_pair + sum(to_y, []) + to_act
 
-    started = work(
-        0, lambda: send_quarters(1, (2,), False), lambda: send_quarters(1, (3,), False)
-    )
-    send_quarters(0, (0,), True)
-    started += work(
-        1, lambda: send_quarters(0, (1,), True), lambda: send_quarters(0, (2, 3), True)
-    )
-    send_quarters(1, range(4), True)
+    started = work(0)
+    send_all(0, True)
+    started += work(1)
+    send_all(1, True)
 
     xt_ref[...] = x_ref[...].T
     for side in range(2):
@@ -398,8 +397,9 @@
         at = pl.ds(pl.multiple_of(start * piece + offset, count), count)
         return act_ref[slab // PIECES, slab % PIECES, :, at]
 
-    gate_ref[...] = dot(xt_ref[...], units(1)).astype(BF16)
-    up_ref[...] = dot(xt_ref[...], units(2)).astype(BF16)
+    pair = dot(xt_ref[...], jnp.concatenate([units(1), units(2)], axis=1)).astype(BF16)
+    gate_ref[...] = pair[:, :count]
+    up_ref[...] = pair[:, count:]
     down_ref[...] = dot(hidt_ref[...], d_ref[...]).astype(BF16)
 
     combined, n = 0.0, 0
@@ -465,11 +465,9 @@
         scratch_shapes=[
             pltpu.VMEM((toks, model_width), BF16),
             pltpu.VMEM((toks, model_width), BF16),
-            pltpu.VMEM((slice_width, hidden), BF16),
-            pltpu.VMEM((slice_width, hidden), BF16),
+            pltpu.VMEM((2 * PIECES, slice_width, 2 * piece), BF16),
             pltpu.VMEM((hidden, slice_width), BF16),
-            pltpu.VMEM((hidden, slice_width), BF16),
-            pltpu.VMEM((hidden, slice_width), BF16),
+            pltpu.VMEM((2 * PIECES, 2 * piece, slice_width), BF16),
             pltpu.VMEM((slice_width, hidden), BF16),
             pltpu.VMEM(handed[1], BF16),
             pltpu.VMEM(handed[1], BF16),
@@ -485,7 +483,7 @@
             pltpu.VMEM(sums, BF16),
             pltpu.VMEM((y_others,) + sums, BF16),
             dma((2,)),
-            dma((3,)),
+            dma((1 + 4 * PIECES,)),
             dma((5,)),
             dma((2 * PARTS,)),
             dma((PARTS,)),

time: 98.4 us -> 96.8 us (0.984)
  Pallas kernels: 97.2 us -> 95.9 us
    pallas_call x1, Pallas kernels: 85.8 us -> 84.5 us  [on_device(): pl.pallas_call(functools.partial(exchange_kernel, experts, heads), out_sh...]
where the time goes in v4:
time: 96.8 us; the launch traced here: 96.6 us
  Pallas kernels  95.9 us (99%)
    pallas_call x1, Pallas kernels, on_device(): pl.pallas_call(functools.partial(exchange_kernel, experts, heads), out_sh...  84.5 us
    pallas_call x1, Pallas kernels, on_device(): pl.pallas_call(functools.partial(finish_kernel, experts), grid=(heads,),...  11.5 us

profile of v4, /device:TPU:0, one launch (start us, length us, event | category | flops | bytes accessed | tf_op | source)
XLA Modules:
  0.0 96.6 jit_solution(3129799063072983603)
XLA Ops:
  0.6 84.5 %shard_map.118 = (bf16[1792,192]{1,0:T(8,128)(2,1)}, bf16[192,1792]{1,0:T(8,128)(2,1)}, bf16[2,1,192,1536]{3,2,1,0:T(8,128)(2,1)}, bf16[1024,192]{1,0:T(8,128)(2...) custom-call(bf16[128,7168]{1,0:T(8,128)(2,1)} %tok_hbm.1, ...), custom_call_target="tpu_custom_call" | custom-call | tf_op jit(solution)/shard_map/pallas_call | solution.py:457
  85.1 11.5 %shard_map.119 = (bf16[128,7168]{1,0:T(8,128)(2,1)}, bf16[128,7168]{1,0:T(8,128)(2,1)}, f32[8,128]{1,0:T(8,128)}, bf16[1792,1024]{1,0:T(8,128)(2,1)}, bf16[1792,...) custom-call(s32[8,128]{1,0:T(8,128)} %bitcast.17, bf16[128,7168]{1,0:T(8,128)(2,1)} %dy_ref.1, ...), custom_call_target="tpu_custom_call" | custom-call | tf_op jit(solution)/shard_map/pallas_call | solution.py:511

commit v5 on v4

--- a/solution.py
+++ b/solution.py
@@ -10,7 +10,7 @@
 CAP = 6
 SPLIT = (4, 2)
 PARTS = len(SPLIT)
-PIECES = 1
+PIECES = 2
 ROWS = 16
 LANES = 128
 MESH = pl.DeviceIdType.MESH
@@ -152,9 +152,10 @@
             (own_back if returning else own_in)(part).start()
         lax.fori_loop(0 if turn else 1, experts, one, 0)
 
-    def send_all(part, returning):
-        for turn in range(heads):
-            send_turn(part, turn, returning)
+    def send_quarters(part, returning, quarters):
+        for q in quarters:
+            for turn in range(q * heads // 4, (q + 1) * heads // 4):
+                send_turn(part, turn, returning)
 
     def fill(part, picked, scale, turn):
         f = form[part]
@@ -192,7 +193,9 @@
             fill(part, picked, scale, turn)
             if part == 0 and turn == 0:
                 pl.semaphore_wait(barrier, total - 1)
-            send_turn(part, turn, False)
+            if part == 0:
+                send_turn(part, turn, False)
+    send_quarters(1, False, (0, 1, 2))
     for copy in weight_copies:
         copy.wait()
 
@@ -245,7 +248,7 @@
     def project(x, d, side, p):
         return dot(x, pair_w[side * PIECES + p]), dot(d, down_t[:, units_of(side, p)])
 
-    def work(part):
+    def work(part, beside_sums, beside_acts):
         f = form[part]
         rows = pl.ds(f.first * total, f.slots * total)
         group_rows = 16 * f.slots
@@ -262,7 +265,7 @@
                 d_ref[at, span] = value[group_rows:]
 
         x, d = x_ref[rows, :], d_ref[rows, :]
-        to_pair, to_y, to_act = [], [], []
+        to_pair, to_y, to_act, sums = [], [], [], []
         for p in range(PIECES):
             ahead, behind = project(x, d, 1 - core, p)
             pair_send[p, rows, : 2 * piece] = ahead
@@ -278,8 +281,6 @@
                 )
             )
             to_pair[-1].start()
-        sums = []
-        for p in range(PIECES):
             mine = jnp.concatenate(project(x, d, core, p), axis=1)
             to_pair[p].wait_recv()
             mine = mine + pair_recv[p, rows]
@@ -298,6 +299,7 @@
                     )
                 )
                 to_y[-1][-1].start()
+        send_quarters(*beside_sums)
         for p in range(PIECES):
             mine = sums[p]
             for q, copy in enumerate(to_y[p]):
@@ -315,6 +317,7 @@
                 )
             )
             to_act[-1].start()
+        send_quarters(*beside_acts)
 
         out, grad = 0.0, 0.0
         for far in range(2):
@@ -342,10 +345,10 @@
             )
         return to_pair + sum(to_y, []) + to_act
 
-    started = work(0)
-    send_all(0, True)
-    started += work(1)
-    send_all(1, True)
+    started = work(0, (1, False, (3,)), (1, False, ()))
+    send_quarters(0, True, (0, 1))
+    started += work(1, (0, True, (2,)), (0, True, (3,)))
+    send_quarters(1, True, range(4))
 
     xt_ref[...] = x_ref[...].T
     for side in range(2):

time: 96.8 us -> 95 us (0.981)
  Pallas kernels: 95.9 us -> 93.5 us
    pallas_call x1, Pallas kernels: 84.5 us -> 82 us  [on_device(): pl.pallas_call(functools.partial(exchange_kernel, experts, heads), out_sh...]
where the time goes in v5:
time: 95 us; the launch traced here: 94.1 us
  Pallas kernels  93.5 us (98%)
    pallas_call x1, Pallas kernels, on_device(): pl.pallas_call(functools.partial(exchange_kernel, experts, heads), out_sh...  82 us
    pallas_call x1, Pallas kernels, on_device(): pl.pallas_call(functools.partial(finish_kernel, experts), grid=(heads,),...  11.5 us

profile of v5, /device:TPU:0, one launch (start us, length us, event | category | flops | bytes accessed | tf_op | source)
XLA Modules:
  0.0 94.1 jit_solution(13667615341881870372)
XLA Ops:
  0.6 82.0 %shard_map.118 = (bf16[1792,192]{1,0:T(8,128)(2,1)}, bf16[192,1792]{1,0:T(8,128)(2,1)}, bf16[2,2,192,768]{3,2,1,0:T(8,128)(2,1)}, bf16[1024,192]{1,0:T(8,128)(2,...) custom-call(bf16[128,7168]{1,0:T(8,128)(2,1)} %tok_hbm.1, ...), custom_call_target="tpu_custom_call" | custom-call | tf_op jit(solution)/shard_map/pallas_call | solution.py:460
  82.7 11.5 %shard_map.119 = (bf16[128,7168]{1,0:T(8,128)(2,1)}, bf16[128,7168]{1,0:T(8,128)(2,1)}, f32[8,128]{1,0:T(8,128)}, bf16[1792,1024]{1,0:T(8,128)(2,1)}, bf16[1792,...) custom-call(s32[8,128]{1,0:T(8,128)} %bitcast.17, bf16[128,7168]{1,0:T(8,128)(2,1)} %dy_ref.1, ...), custom_call_target="tpu_custom_call" | custom-call | tf_op jit(solution)/shard_map/pallas_call | solution.py:514
